TPU v7x, 32 devices: a whole 2x2x4 slice. The times are simulated.
32 devices in a mesh: dom: 4 (over y, x), depth: 8 (over z, core).
Axes of the slice: x: 2, y: 2, z: 4, core: 2. Of those that a mesh axis runs over, the one named last changes fastest.
Arguments:
- head: float32 [8, 256, 512], P('depth', 'dom'), may hold values from -1.5 to 0.3
- water_prev: float32 [8, 256, 512], P('depth', 'dom'), may hold values from 0.05 to 0.4
- alpha: float32 [8, 256, 512], P('depth', 'dom'), may hold values from 0.3 to 3
- shape_n: float32 [8, 256, 512], P('depth', 'dom'), may hold values from 1.3 to 3
- theta_r: float32 [8, 256, 512], P('depth', 'dom'), may hold values from 0.02 to 0.1
- theta_s: float32 [8, 256, 512], P('depth', 'dom'), may hold values from 0.35 to 0.5
- sat_cond: float32 [8, 256, 512], P('depth', 'dom'), may hold values from 0.5 to 5
- refine: int32 [256], P('dom'), may hold values from 0 to 8
- destination: int32 [256], P('dom'), may hold values from 0 to 255, as said below
- neighbours: int32 [256, 4, 4], P('dom'), may hold values from -1 to 255, as said below
Outputs:
- new_head: float32 [8, 256, 512], P('depth', 'dom')
- residual: float32 [8, 256, 512], P('depth', 'dom')
Inputs may be any that keep to these rules, and one draw needn't show every extreme that they name: destination is a permutation of the 256 positions, position p on device p // 64. The blocks of each device go to exactly 3 other devices, exactly 4 to each; its other blocks stay on it. neighbours[p, f] lists the new positions beyond lateral face f of new block p: all four entries -1 where there is no neighbour; one block in entry 0 and -1 in the rest for a face of equal size; or four finer blocks, entry (a // 4) * 2 + b // 4 for face cell (a, b). Every listed block lies at most 16 positions from p, some at exactly 16.
All inputs are finite; a program needn't handle non-finite values.
Results may differ from a plain program's by a relative error of at most 0.0003.
Values sent between devices are 32-bit elements; how exact they have to be, the bound alone decides.
A program may use at most 128 MiB of HBM per device.

v0:
```python
import jax
import jax.numpy as jnp
import numpy as np
from jax import lax
from jax.sharding import PartitionSpec as P

inv_step = 4.0
exact = lax.Precision.HIGHEST


def with_halo(x, sides, width):
    for axis, dim in sides:
        peers, length = (lax.axis_size(axis), x.shape[dim])
        up = [(i, (i + 1) % peers) for i in range(peers - 1)]
        down = [(j, i) for i, j in up]
        last = lax.slice_in_dim(x, length - width, length, axis=dim)
        initial = lax.slice_in_dim(x, 0, width, axis=dim)
        before = lax.ppermute(last, axis, up)
        after = lax.ppermute(initial, axis, down)
        x = jnp.concatenate([before, x, after], axis=dim)
    return x


def axis_table(stride, bit, smooth):
    table = np.zeros((512, 512), np.float32)
    for cell in range(512):
        fine = cell // stride % 8
        base = cell - fine * stride
        half = fine // 2
        if smooth:
            if fine % 2 == 0:
                table[base + max(4 * bit + half - 1, 0) * stride, cell] += 0.25
                table[base + (4 * bit + half) * stride, cell] += 0.75
            else:
                table[base + (4 * bit + half) * stride, cell] += 0.75
                table[base + min(4 * bit + half + 1, 7) * stride, cell] += 0.25
        else:
            table[base + (4 * bit + half) * stride, cell] = 1.0
    return table


def face_cells(face):
    listed = []
    for first in range(8):
        for second in range(8):
            if face == 0:
                listed.append(first * 8 + second)
            elif face == 1:
                listed.append(448 + first * 8 + second)
            elif face == 2:
                listed.append(first * 64 + second)
            else:
                listed.append(first * 64 + 56 + second)
    return listed


def plane_cells(level_k):
    return [first * 64 + second * 8 + level_k for first in range(8) for second in range(8)]


def take_faces(offset_k):
    table = np.zeros((512, 512), np.float32)
    for face in range(4):
        for spot, cell in enumerate(face_cells(face)):
            table[cell, face * 128 + offset_k + spot] = 1.0
    return table


def take_plane(level_k, offset_k):
    table = np.zeros((512, 128), np.float32)
    for spot, cell in enumerate(plane_cells(level_k)):
        table[cell, offset_k + spot] = 1.0
    return table


def put_cells(listed):
    table = np.zeros((64, 512), np.float32)
    for spot, cell in enumerate(listed):
        table[spot, cell] = 1.0
    return table


def quarter_tables():
    table = np.zeros((4, 4, 128, 128), np.float32)
    for part_k in range(2):
        for first in range(8):
            for second in range(8):
                quarter = first // 4 * 2 + second // 4
                for pair in range(4):
                    source = (
                        part_k * 64
                        + (2 * (first % 4) + pair // 2) * 8
                        + 2 * (second % 4)
                        + pair % 2
                    )
                    table[pair, quarter, source, part_k * 64 + first * 8 + second] = 1.0
    return table


def interior_mask(stride, upward):
    cells = np.arange(512)
    index = cells // stride % 8
    return index < 7 if upward else index > 0


def select(values, table):
    return jnp.einsum("...c,cd->...d", values, jnp.asarray(table), precision=exact)


def adapt(fields, flags, smooth):
    octant = jnp.maximum(flags - 1, 0)
    current = fields
    for stride, bits in ((64, octant // 4), (8, octant // 2 % 2), (1, octant % 2)):
        first = select(current, axis_table(stride, 0, smooth))
        second = select(current, axis_table(stride, 1, smooth))
        current = jnp.where((bits == 1).reshape(1, -1, 1), second, first)
    return jnp.where((flags == 0).reshape(1, -1, 1), fields, current)


def closure(head_cell, cell_alpha, cell_shape, cell_resid, cell_sat, cell_cond):
    expo = 1.0 - 1.0 / cell_shape
    ratio = jnp.power(cell_alpha * jnp.maximum(-head_cell, 0.0), cell_shape)
    saturation = jnp.power(1.0 + ratio, -expo)
    water = cell_resid + (cell_sat - cell_resid) * saturation
    inner = 1.0 - jnp.power(ratio / (1.0 + ratio), expo)
    conduct = cell_cond * jnp.sqrt(saturation) * inner * inner
    return (water, conduct)


def ghost_values(wide, table_nb):
    rows = wide.reshape(-1, 128)
    safe = jnp.maximum(table_nb, 0)
    opposite = jnp.array([1, 0, 3, 2], jnp.int32).reshape(1, 4, 1)
    picked = rows[safe * 4 + opposite]
    conform = picked[:, :, 0]
    tables = quarter_tables()
    terms = [
        jnp.einsum("bfex,exy->bfy", picked, jnp.asarray(tables[pair]), precision=exact)
        for pair in range(4)
    ]
    hanging = 0.25 * (terms[0] + terms[1] + terms[2] + terms[3])
    count = jnp.sum((table_nb >= 0).astype(jnp.int32), axis=2)
    value = jnp.where((count == 4)[:, :, None], hanging, conform)
    present = (count > 0).astype(jnp.float32)
    return (value, present)


def moved_by(values, stride, upward):
    blocks = values.shape[0]
    empty = jnp.zeros((blocks, stride), values.dtype)
    if upward:
        return jnp.concatenate([values[:, stride:], empty], axis=1)
    return jnp.concatenate([empty, values[:, : 512 - stride]], axis=1)


def balance(
    head_cell,
    water,
    conduct,
    prior,
    cell_alpha,
    cell_resid,
    cell_sat,
    lat_value,
    lat_on,
    below,
    above,
    low_on,
    high_on,
):
    plans = []
    for face, stride, upward in ((0, 64, False), (1, 64, True), (2, 8, False), (3, 8, True)):
        cells_table = put_cells(face_cells(face))
        plans.append(
            (
                select(lat_value[:, face, :64], cells_table),
                select(lat_value[:, face, 64:], cells_table),
                lat_on[:, face : face + 1],
                stride,
                upward,
                0.0,
            )
        )
    low_table = put_cells(plane_cells(0))
    high_table = put_cells(plane_cells(7))
    plans.append(
        (select(below[:, :64], low_table), select(below[:, 64:], low_table), low_on, 1, False, -1.0)
    )
    plans.append(
        (
            select(above[:, :64], high_table),
            select(above[:, 64:], high_table),
            high_on,
            1,
            True,
            1.0,
        )
    )
    flux = jnp.zeros_like(head_cell)
    total = jnp.zeros_like(head_cell)
    for ghost_h, ghost_k, plane_on, stride, upward, lift in plans:
        inside = jnp.asarray(interior_mask(stride, upward)).reshape(1, 512)
        near_h = jnp.where(inside, moved_by(head_cell, stride, upward), ghost_h)
        near_k = jnp.where(inside, moved_by(conduct, stride, upward), ghost_k)
        near_on = jnp.where(inside, 1.0, plane_on * jnp.ones_like(head_cell))
        face_k = near_on * 0.5 * (conduct + near_k)
        flux = flux + face_k * (near_h - head_cell + lift)
        total = total + face_k
    resid = inv_step * (water - prior) - flux
    diagonal = inv_step * (cell_sat - cell_resid) * cell_alpha + total
    return (resid, diagonal)


def relocate(stacked, destination):
    fields, blocks, cells = stacked.shape
    peers = lax.axis_size("dom")
    rank_me = lax.axis_index("dom")
    room = blocks // 16
    owner = destination // blocks
    spot = destination % blocks
    remote = owner != rank_me
    picked = ((owner[:, None] == jnp.arange(peers)[None, :]) & remote[:, None]).astype(jnp.int32)
    order = jnp.sum(jnp.cumsum(picked, axis=0) * picked, axis=1) - 1
    slot = jnp.where(remote, owner * room + order, peers * room)
    packed = (
        jnp.zeros((fields, peers * room + 1, cells), stacked.dtype)
        .at[:, slot]
        .set(stacked)[:, : peers * room]
    )
    places = jnp.full((1, peers * room + 1), -1, jnp.int32).at[0, slot].set(spot)[:, : peers * room]
    packed, places = (
        lax.all_to_all(packed, "dom", split_axis=1, concat_axis=1, tiled=True),
        lax.all_to_all(places, "dom", split_axis=1, concat_axis=1, tiled=True),
    )
    target = jnp.concatenate(
        [jnp.where(remote, blocks, spot), jnp.where(places[0] >= 0, places[0], blocks)]
    )
    values = jnp.concatenate([stacked, packed], axis=1)
    return (
        jnp.zeros((fields, blocks + 1, cells), stacked.dtype).at[:, target].set(values)[:, :blocks]
    )


def evaluate(
    head_cell,
    prior,
    cell_alpha,
    cell_shape,
    cell_resid,
    cell_sat,
    cell_cond,
    local_nb,
    low_on,
    high_on,
    reach,
):
    water, conduct = closure(head_cell, cell_alpha, cell_shape, cell_resid, cell_sat, cell_cond)
    faces = select(head_cell, take_faces(0)) + select(conduct, take_faces(64))
    wide = with_halo(faces, (("dom", 0),), reach)
    lat_value, lat_on = ghost_values(wide, local_nb)
    bottom = select(head_cell, take_plane(0, 0)) + select(conduct, take_plane(0, 64))
    top = select(head_cell, take_plane(7, 0)) + select(conduct, take_plane(7, 64))
    tall = with_halo(jnp.stack([bottom, top]), (("depth", 0),), 1)
    return balance(
        head_cell,
        water,
        conduct,
        prior,
        cell_alpha,
        cell_resid,
        cell_sat,
        lat_value,
        lat_on,
        tall[0],
        tall[3],
        low_on,
        high_on,
    )


def on_device(
    head, water_prev, alpha, shape_n, theta_r, theta_s, sat_cond, refine, destination, neighbours
):
    blocks = head.shape[1]
    smooth_part = adapt(jnp.concatenate([head, water_prev], axis=0), refine, True)
    plain_part = adapt(
        jnp.concatenate([alpha, shape_n, theta_r, theta_s, sat_cond], axis=0), refine, False
    )
    settled = relocate(jnp.concatenate([smooth_part, plain_part], axis=0), destination)
    start, prior, cell_alpha, cell_shape, cell_resid, cell_sat, cell_cond = [
        settled[number] for number in range(7)
    ]
    level = lax.axis_index("depth")
    low_on = (level > 0).astype(jnp.float32)
    high_on = (level < lax.axis_size("depth") - 1).astype(jnp.float32)
    reach = blocks // 4
    offset = lax.axis_index("dom") * blocks - reach
    local_nb = jnp.where(neighbours >= 0, neighbours - offset, -1)
    resid, diagonal = evaluate(
        start,
        prior,
        cell_alpha,
        cell_shape,
        cell_resid,
        cell_sat,
        cell_cond,
        local_nb,
        low_on,
        high_on,
        reach,
    )
    new_head = start - resid / diagonal
    final, unused = evaluate(
        new_head,
        prior,
        cell_alpha,
        cell_shape,
        cell_resid,
        cell_sat,
        cell_cond,
        local_nb,
        low_on,
        high_on,
        reach,
    )
    return (new_head[None], final[None])


def solution(mesh):
    placed = (
        P("depth", "dom", None),
        P("depth", "dom", None),
        P("depth", "dom", None),
        P("depth", "dom", None),
        P("depth", "dom", None),
        P("depth", "dom", None),
        P("depth", "dom", None),
        P("dom"),
        P("dom"),
        P("dom", None, None),
    )
    return jax.shard_map(
        on_device,
        mesh=mesh,
        in_specs=placed,
        out_specs=(P("depth", "dom", None), P("depth", "dom", None)),
        check_vma=False,
    )
```

profile of v0, /device:TPU:21, one launch (start us, length us, event | category | flops | bytes accessed | tf_op | source)
XLA Modules:
  0.0 109.2 jit_solution(5718164986902517227)
XLA Ops:
  3.3 3.7 %all-to-all-start = ((s32[1,4,4]{2,0,1:T(1,128)}), s32[1,4,4]{2,0,1:T(1,128)S(1)}, u32[]{:S(2)}, u32[]{:S(2)}) async-start(s32[1,4,4]{2,0,1:T(1,128)} %bitcast.2), calls=%async_computation | async-start | bytes 4096 | tf_op jit(solution)/shard_map/all_to_all | solution.py:233
  11.4 1.2 %fusion.132 = f32[5,64,512]{2,1,0:T(8,128)S(1)} fusion(f32[5,64,512]{2,1,0:T(8,128)S(1)} %constant_dynamic-update-slice_fusion.2, f32[512,512,1]{1,0,2:T(8,128)S(1)} %copy-done.46), kind=kOutput, calls=%fused_computation.263 | convolution fusion | flops 1006632960 | bytes 2359296 | tf_op jit(solution)/shard_map/...c,cd->...d/dot_general | solution.py:107
  12.7 1.3 %convolution_select_fusion.2 = f32[5,64,512]{2,1,0:T(8,128)S(1)} fusion(f32[5,64,512]{2,1,0:T(8,128)S(1)} %fusion.132, f32[5,64,512]{2,1,0:T(8,128)S(1)} %constant_dynamic-update-slice_fusion.2, f32[512,512,1]{1,0,2:T(8,128)S(1)} %copy-done.28, pred[64]{0:T(512)(128)(4,1)S(1)} %get-tuple-element.52), kind=kOutput, calls=%fused_computation.8 | convolution fusion | flops 1006796800 | bytes 3014720 | tf_op jit(solution)/shard_map/...c,cd->...d/dot_general | solution.py:107
  13.9 1.2 %fusion.133 = f32[5,64,512]{2,1,0:T(8,128)S(1)} fusion(f32[5,64,512]{2,1,0:T(8,128)S(1)} %convolution_select_fusion.2, f32[512,512,1]{1,0,2:T(8,128)S(1)} %copy-done.45), kind=kOutput, calls=%fused_computation.264 | convolution fusion | flops 1006632960 | bytes 2359296 | tf_op jit(solution)/shard_map/...c,cd->...d/dot_general | solution.py:107
  15.2 1.3 %convolution_select_fusion.1 = f32[5,64,512]{2,1,0:T(8,128)S(1)} fusion(f32[5,64,512]{2,1,0:T(8,128)S(1)} %fusion.133, f32[5,64,512]{2,1,0:T(8,128)S(1)} %convolution_select_fusion.2, f32[512,512,1]{1,0,2:T(8,128)S(1)} %copy-done.27, pred[64]{0:T(512)(128)(4,1)S(1)} %get-tuple-element.53), kind=kOutput, calls=%fused_computation.7 | convolution fusion | flops 1006796800 | bytes 3014720 | tf_op jit(solution)/shard_map/...c,cd->...d/dot_general | solution.py:107
  16.5 1.2 %fusion.134 = f32[5,64,512]{2,1,0:T(8,128)S(1)} fusion(f32[5,64,512]{2,1,0:T(8,128)S(1)} %convolution_select_fusion.1, f32[512,512,1]{1,0,2:T(8,128)S(1)} %copy-done.44), kind=kOutput, calls=%fused_computation.265 | convolution fusion | flops 1006632960 | bytes 2359296 | tf_op jit(solution)/shard_map/...c,cd->...d/dot_general | solution.py:107
  23.9 1.3 %fusion = f32[5,64,512]{2,1,0:T(8,128)S(1)} fusion(f32[5,64,512]{2,1,0:T(8,128)S(1)} %constant_dynamic-update-slice_fusion.2, f32[5,64,512]{2,1,0:T(8,128)S(1)} %fusion.134, f32[5,64,512]{2,1,0:T(8,128)S(1)} %convolution_select_fusion.1, f32[512,512,1]{1,0,2:T(8,128)S(1)} %copy-done.52, pred[64]{0:T(512)(128)(4,1)S(1)} %get-tuple-element.54, ...), kind=kOutput, calls=%fused_computation.6 | convolution fusion | flops 1006960640 | bytes 3670144 | tf_op jit(solution)/shard_map/...c,cd->...d/dot_general | solution.py:107
  26.6 2.8 %scatter_fusion = f32[7,17,512]{2,0,1:T(8,128)S(1)} fusion(f32[7,17,512]{2,0,1:T(8,128)S(1)} %broadcast_in_dim.271, s32[64]{0:T(128)S(1)} %compare_select_fusion.3, f32[64,7,512]{2,1,0:T(8,128)S(1)} %copy.112), kind=kCustom, calls=%fused_computation.3 | custom fusion | bytes 2752768 | tf_op jit(solution)/shard_map/scatter | solution.py:228
  32.1 3.6 %all-to-all-start.1 = ((f32[7,16,512]{2,0,1:T(8,128)}), f32[7,16,512]{2,0,1:T(8,128)S(1)}, u32[]{:S(2)}, u32[]{:S(2)}) async-start(f32[7,16,512]{2,0,1:T(8,128)} %slice.286), calls=%async_computation.1 | async-start | bytes 524288 | tf_op jit(solution)/shard_map/all_to_all | solution.py:232
  37.1 2.7 %all-to-all-done.1 = f32[7,16,512]{2,0,1:T(8,128)S(1)} async-done(((f32[7,16,512]{2,0,1:T(8,128)}), f32[7,16,512]{2,0,1:T(8,128)S(1)}, u32[]{:S(2)}, u32[]{:S(2)}) %all-to-all-start.1) | async-done | bytes 229408 | tf_op jit(solution)/shard_map/all_to_all | solution.py:232
  40.8 3.0 %scatter_fusion.1 = f32[7,65,512]{2,0,1:T(8,128)S(1)} fusion(f32[7,65,512]{2,0,1:T(8,128)S(1)} %broadcast_in_dim.259, s32[80]{0:T(128)S(1)} %fusion.110, f32[80,7,512]{2,1,0:T(8,128)S(1)} %copy.114), kind=kCustom, calls=%fused_computation.4 | custom fusion | bytes 3440960 | tf_op jit(solution)/shard_map/scatter | solution.py:240
  43.8 1.4 %fusion.114 = (f32[1,64,512]{2,0,1:T(1,128)}, f32[1,64,512]{2,0,1:T(1,128)S(1)}, f32[1,64,512]{2,0,1:T(1,128)S(1)}, f32[1,64,512]{2,0,1:T(1,128)}, f32[1,64,512]...) fusion(f32[7,65,512]{2,0,1:T(8,128)S(1)} %scatter_fusion.1), kind=kLoop, calls=%fused_computation.245 | loop fusion | bytes 1835008 | tf_op jit(solution)/shard_map/slice | solution.py:291
  50.2 1.9 %collective-permute-start = (f32[16,512]{1,0:T(8,128)S(1)}, f32[16,512]{1,0:T(8,128)S(1)}, u32[]{:S(2)}, u32[]{:S(2)}) collective-permute-start(f32[16,512]{1,0:T(8,128)S(1)} %get-tuple-element.41), channel_id=1, source_target_pairs={{0,8},{8,16},{16,24},{1,9},{9,17},{17,25},{2,10},{10,18},{18,26},{... | collective-permute-start | bytes 98312 | tf_op jit(solution)/shard_map/ppermute | solution.py:18
  52.1 4.3 %collective-permute-start.1 = (f32[16,512]{1,0:T(8,128)S(1)}, f32[16,512]{1,0:T(8,128)S(1)}, u32[]{:S(2)}, u32[]{:S(2)}) collective-permute-start(f32[16,512]{1,0:T(8,128)S(1)} %get-tuple-element.42), channel_id=1, source_target_pairs={{8,0},{16,8},{24,16},{9,1},{17,9},{25,17},{10,2},{18,10},{26,18},{... | collective-permute-start | bytes 98312 | tf_op jit(solution)/shard_map/ppermute | solution.py:19
  57.6 6.0 %collective-permute-start.2 = (f32[1,64,128]{2,1,0:T(8,128)}, f32[1,64,128]{2,1,0:T(8,128)S(1)}, u32[]{:S(2)}, u32[]{:S(2)}) collective-permute-start(f32[1,64,128]{2,1,0:T(8,128)} %fusion.82), channel_id=1, source_target_pairs={{0,1},{1,2},{2,3},{3,4},{4,5},{5,6},{6,7},{8,9},{9,10},{10,11},{11... | collective-permute-start | bytes 98312 | tf_op jit(solution)/shard_map/ppermute | solution.py:18
  64.8 1.9 %collective-permute-start.3 = (f32[1,64,128]{2,1,0:T(8,128)}, f32[1,64,128]{2,1,0:T(8,128)S(1)}, u32[]{:S(2)}, u32[]{:S(2)}) collective-permute-start(f32[1,64,128]{2,1,0:T(8,128)} %fusion.81), channel_id=1, source_target_pairs={{1,0},{2,1},{3,2},{4,3},{5,4},{6,5},{7,6},{9,8},{10,9},{11,10},{12... | collective-permute-start | bytes 98312 | tf_op jit(solution)/shard_map/ppermute | solution.py:19
  66.8 3.0 %gather_fusion = f32[1024,128]{1,0:T(8,128)S(1)} fusion(f32[384,128]{1,0:T(8,128)S(1)} %reshape.135, s32[1024]{0:T(1024)S(1)} %broadcast_clamp_fusion), kind=kCustom, calls=%fused_computation | custom fusion | bytes 1052672 | tf_op jit(solution)/shard_map/gather | solution.py:134
  76.9 1.4 %multiply_multiply_fusion = (f32[64,512]{1,0:T(8,128)S(1)}, f32[64,512]{1,0:T(8,128)S(1)}) fusion(f32[1,64,512]{2,0,1:T(1,128)S(1)} %copy-done.20, f32[1,64,512]{2,0,1:T(1,128)S(1)} %copy-done.12, f32[1,64,512]{2,0,1:T(1,128)S(1)} %copy-done.15, f32[64,512]{1,0:T(8,128)S(1)} %get-tuple-element.7, f32[64,512]{1,0:T(8,128)S(1)} %fusion.32, ...), kind=kOutput, calls=%fused_computation.144 | convolution fusion | flops 26476544 | bytes 2916864 | tf_op jit(solution)/shard_map/...c,cd->...d/dot_general | solution.py:107
  84.9 1.9 %collective-permute-start.4 = (f32[16,512]{1,0:T(8,128)S(1)}, f32[16,512]{1,0:T(8,128)S(1)}, u32[]{:S(2)}, u32[]{:S(2)}) collective-permute-start(f32[16,512]{1,0:T(8,128)S(1)} %get-tuple-element.27), channel_id=1, source_target_pairs={{0,8},{8,16},{16,24},{1,9},{9,17},{17,25},{2,10},{10,18},{18,26},{... | collective-permute-start | bytes 98312 | tf_op jit(solution)/shard_map/ppermute | solution.py:18
  86.9 4.3 %collective-permute-start.5 = (f32[16,512]{1,0:T(8,128)S(1)}, f32[16,512]{1,0:T(8,128)S(1)}, u32[]{:S(2)}, u32[]{:S(2)}) collective-permute-start(f32[16,512]{1,0:T(8,128)S(1)} %get-tuple-element.28), channel_id=1, source_target_pairs={{8,0},{16,8},{24,16},{9,1},{17,9},{25,17},{10,2},{18,10},{26,18},{... | collective-permute-start | bytes 98312 | tf_op jit(solution)/shard_map/ppermute | solution.py:19
  91.4 4.2 %collective-permute-start.6 = (f32[1,64,128]{2,1,0:T(8,128)S(1)}, f32[1,64,128]{2,1,0:T(8,128)S(1)}, u32[]{:S(2)}, u32[]{:S(2)}) collective-permute-start(f32[1,64,128]{2,1,0:T(8,128)S(1)} %fusion.80), channel_id=1, source_target_pairs={{0,1},{1,2},{2,3},{3,4},{4,5},{5,6},{6,7},{8,9},{9,10},{10,11},{11... | collective-permute-start | bytes 98312 | tf_op jit(solution)/shard_map/ppermute | solution.py:18
  95.9 1.9 %collective-permute-start.7 = (f32[1,64,128]{2,1,0:T(8,128)S(1)}, f32[1,64,128]{2,1,0:T(8,128)S(1)}, u32[]{:S(2)}, u32[]{:S(2)}) collective-permute-start(f32[1,64,128]{2,1,0:T(8,128)S(1)} %fusion.79), channel_id=1, source_target_pairs={{1,0},{2,1},{3,2},{4,3},{5,4},{6,5},{7,6},{9,8},{10,9},{11,10},{12... | collective-permute-start | bytes 98312 | tf_op jit(solution)/shard_map/ppermute | solution.py:19
  97.9 3.1 %gather_fusion.1 = f32[1024,128]{1,0:T(8,128)S(1)} fusion(f32[384,128]{1,0:T(8,128)S(1)} %reshape.136, s32[1024]{0:T(1024)S(1)} %broadcast_clamp_fusion), kind=kCustom, calls=%fused_computation.1 | custom fusion | bytes 1052672 | tf_op jit(solution)/shard_map/gather | solution.py:134
  107.8 1.4 %fusion.45 = f32[1,64,512]{2,1,0:T(8,128)} fusion(f32[64,512]{1,0:T(8,128)S(1)} %fusion.66, f32[64,512]{1,0:T(8,128)S(1)} %fusion.61, f32[64,512]{1,0:T(8,128)S(1)} %fusion.57, f32[64,512]{1,0:T(8,128)S(1)} %fusion.53, f32[64,512]{1,0:T(8,128)S(1)} %fusion.49, f32[64,512]{1,0:T(8,128)S(1)} %fusion.46, f32[64,512]{1,0:T(8,128)S(1)} %get-tuple-element.55, ...), kind=kOutput, calls=%fused_computation.91 | convolution fusion | flops 25952256 | bytes 2130944 | tf_op jit(solution)/shard_map/...c,cd->...d/dot_general | solution.py:107
  (322 shorter events, 46.4 us)
Async XLA Ops:
  0.6 10.7 %copy-start.46 = (f32[512,512,1]{1,0,2:T(8,128)S(1)}, f32[512,512,1]{1,0,2:T(8,128)}, u32[]{:S(2)}) copy-start(f32[512,512,1]{1,0,2:T(8,128)} %constant.305) | copy-start | bytes 3145732
  0.6 10.7 %copy-start.77 = (f32[1,64,512]{2,1,0:T(8,128)S(1)}, f32[1,64,512]{2,1,0:T(8,128)}, u32[]{:S(2)}) copy-start(f32[1,64,512]{2,1,0:T(8,128)} %param.73) | copy-start | bytes 393220
  0.7 10.7 %copy-start.78 = (f32[1,64,512]{2,1,0:T(8,128)S(1)}, f32[1,64,512]{2,1,0:T(8,128)}, u32[]{:S(2)}) copy-start(f32[1,64,512]{2,1,0:T(8,128)} %param.74) | copy-start | bytes 393220
  3.3 28.8 %all-to-all-start = ((s32[1,4,4]{2,0,1:T(1,128)}), s32[1,4,4]{2,0,1:T(1,128)S(1)}, u32[]{:S(2)}, u32[]{:S(2)}) async-start(s32[1,4,4]{2,0,1:T(1,128)} %bitcast.2), calls=%async_computation | async-start | bytes 4096 | tf_op jit(solution)/shard_map/all_to_all | solution.py:233
  26.6 3.6 %copy-start.84 = (s32[64,4,4]{0,2,1:T(4,128)S(1)}, s32[64,4,4]{0,2,1:T(4,128)}, u32[]{:S(2)}) copy-start(s32[64,4,4]{0,2,1:T(4,128)} %param.77) | copy-start | bytes 12292
  26.6 5.4 %copy-start.81 = (pred[512]{0:T(512)(128)(4,1)S(1)}, pred[512]{0:T(512)(128)(4,1)}, u32[]{:S(2)}) copy-start(pred[512]{0:T(512)(128)(4,1)} %constant.237.clone) | copy-start | bytes 1540
  26.6 5.4 %copy-start.80 = (pred[512]{0:T(512)(128)(4,1)S(1)}, pred[512]{0:T(512)(128)(4,1)}, u32[]{:S(2)}) copy-start(pred[512]{0:T(512)(128)(4,1)} %constant.238.clone) | copy-start | bytes 1540
  32.1 7.7 %all-to-all-start.1 = ((f32[7,16,512]{2,0,1:T(8,128)}), f32[7,16,512]{2,0,1:T(8,128)S(1)}, u32[]{:S(2)}, u32[]{:S(2)}) async-start(f32[7,16,512]{2,0,1:T(8,128)} %slice.286), calls=%async_computation.1 | async-start | bytes 524288 | tf_op jit(solution)/shard_map/all_to_all | solution.py:232
  48.6 7.8 %copy-start.50 = (f32[512,128]{1,0:T(8,128)S(1)}, f32[512,128]{1,0:T(8,128)}, u32[]{:S(2)}) copy-start(f32[512,128]{1,0:T(8,128)} %constant.225.clone) | copy-start | bytes 786436
  49.4 7.3 %copy-start.37 = (f32[512,128]{1,0:T(8,128)S(1)}, f32[512,128]{1,0:T(8,128)}, u32[]{:S(2)}) copy-start(f32[512,128]{1,0:T(8,128)} %constant.226.clone) | copy-start | bytes 786436
  49.4 14.2 %copy-start.48 = (f32[512,128]{1,0:T(8,128)S(1)}, f32[512,128]{1,0:T(8,128)}, u32[]{:S(2)}) copy-start(f32[512,128]{1,0:T(8,128)} %constant.223.clone) | copy-start | bytes 786436
  49.4 14.5 %copy-start.35 = (f32[512,128]{1,0:T(8,128)S(1)}, f32[512,128]{1,0:T(8,128)}, u32[]{:S(2)}) copy-start(f32[512,128]{1,0:T(8,128)} %constant.224.clone) | copy-start | bytes 786436
  50.2 16.5 %collective-permute-start = (f32[16,512]{1,0:T(8,128)S(1)}, f32[16,512]{1,0:T(8,128)S(1)}, u32[]{:S(2)}, u32[]{:S(2)}) collective-permute-start(f32[16,512]{1,0:T(8,128)S(1)} %get-tuple-element.41), channel_id=1, source_target_pairs={{0,8},{8,16},{16,24},{1,9},{9,17},{17,25},{2,10},{10,18},{18,26},{... | collective-permute-start | bytes 98312 | tf_op jit(solution)/shard_map/ppermute | solution.py:18
  52.1 14.6 %collective-permute-start.1 = (f32[16,512]{1,0:T(8,128)S(1)}, f32[16,512]{1,0:T(8,128)S(1)}, u32[]{:S(2)}, u32[]{:S(2)}) collective-permute-start(f32[16,512]{1,0:T(8,128)S(1)} %get-tuple-element.42), channel_id=1, source_target_pairs={{8,0},{16,8},{24,16},{9,1},{17,9},{25,17},{10,2},{18,10},{26,18},{... | collective-permute-start | bytes 98312 | tf_op jit(solution)/shard_map/ppermute | solution.py:19
  57.6 17.5 %collective-permute-start.2 = (f32[1,64,128]{2,1,0:T(8,128)}, f32[1,64,128]{2,1,0:T(8,128)S(1)}, u32[]{:S(2)}, u32[]{:S(2)}) collective-permute-start(f32[1,64,128]{2,1,0:T(8,128)} %fusion.82), channel_id=1, source_target_pairs={{0,1},{1,2},{2,3},{3,4},{4,5},{5,6},{6,7},{8,9},{9,10},{10,11},{11... | collective-permute-start | bytes 98312 | tf_op jit(solution)/shard_map/ppermute | solution.py:18
  64.8 11.0 %collective-permute-start.3 = (f32[1,64,128]{2,1,0:T(8,128)}, f32[1,64,128]{2,1,0:T(8,128)S(1)}, u32[]{:S(2)}, u32[]{:S(2)}) collective-permute-start(f32[1,64,128]{2,1,0:T(8,128)} %fusion.81), channel_id=1, source_target_pairs={{1,0},{2,1},{3,2},{4,3},{5,4},{6,5},{7,6},{9,8},{10,9},{11,10},{12... | collective-permute-start | bytes 98312 | tf_op jit(solution)/shard_map/ppermute | solution.py:19
  78.3 29.3 %copy-start = (f32[64,512]{1,0:T(8,128)}, f32[64,512]{1,0:T(8,128)S(1)}, u32[]{:S(2)}) copy-start(f32[64,512]{1,0:T(8,128)S(1)} %get-tuple-element.56) | copy-start | bytes 393220
  83.1 8.0 %copy-start.38 = (f32[512,128]{1,0:T(8,128)S(1)}, f32[512,128]{1,0:T(8,128)}, u32[]{:S(2)}) copy-start(f32[512,128]{1,0:T(8,128)} %constant.226.clone) | copy-start | bytes 786436
  83.9 11.7 %copy-start.36 = (f32[512,128]{1,0:T(8,128)S(1)}, f32[512,128]{1,0:T(8,128)}, u32[]{:S(2)}) copy-start(f32[512,128]{1,0:T(8,128)} %constant.224.clone) | copy-start | bytes 786436
  84.9 12.9 %collective-permute-start.4 = (f32[16,512]{1,0:T(8,128)S(1)}, f32[16,512]{1,0:T(8,128)S(1)}, u32[]{:S(2)}, u32[]{:S(2)}) collective-permute-start(f32[16,512]{1,0:T(8,128)S(1)} %get-tuple-element.27), channel_id=1, source_target_pairs={{0,8},{8,16},{16,24},{1,9},{9,17},{17,25},{2,10},{10,18},{18,26},{... | collective-permute-start | bytes 98312 | tf_op jit(solution)/shard_map/ppermute | solution.py:18
  86.9 11.0 %collective-permute-start.5 = (f32[16,512]{1,0:T(8,128)S(1)}, f32[16,512]{1,0:T(8,128)S(1)}, u32[]{:S(2)}, u32[]{:S(2)}) collective-permute-start(f32[16,512]{1,0:T(8,128)S(1)} %get-tuple-element.28), channel_id=1, source_target_pairs={{8,0},{16,8},{24,16},{9,1},{17,9},{25,17},{10,2},{18,10},{26,18},{... | collective-permute-start | bytes 98312 | tf_op jit(solution)/shard_map/ppermute | solution.py:19
  91.4 14.6 %collective-permute-start.6 = (f32[1,64,128]{2,1,0:T(8,128)S(1)}, f32[1,64,128]{2,1,0:T(8,128)S(1)}, u32[]{:S(2)}, u32[]{:S(2)}) collective-permute-start(f32[1,64,128]{2,1,0:T(8,128)S(1)} %fusion.80), channel_id=1, source_target_pairs={{0,1},{1,2},{2,3},{3,4},{4,5},{5,6},{6,7},{8,9},{9,10},{10,11},{11... | collective-permute-start | bytes 98312 | tf_op jit(solution)/shard_map/ppermute | solution.py:18
  95.9 11.2 %collective-permute-start.7 = (f32[1,64,128]{2,1,0:T(8,128)S(1)}, f32[1,64,128]{2,1,0:T(8,128)S(1)}, u32[]{:S(2)}, u32[]{:S(2)}) collective-permute-start(f32[1,64,128]{2,1,0:T(8,128)S(1)} %fusion.79), channel_id=1, source_target_pairs={{1,0},{2,1},{3,2},{4,3},{5,4},{6,5},{7,6},{9,8},{10,9},{11,10},{12... | collective-permute-start | bytes 98312 | tf_op jit(solution)/shard_map/ppermute | solution.py:19
  97.9 3.8 %copy-start.32 = (f32[4,128,128,1]{2,1,0,3:T(8,128)S(1)}, f32[4,128,128,1]{2,1,0,3:T(8,128)}, u32[]{:S(2)}) copy-start(f32[4,128,128,1]{2,1,0,3:T(8,128)} %constant.313) | copy-start | bytes 786436
  (90 other events, 134.6 us)
where the time goes:
time: 110 us; the launch traced here: 109 us
  starting transfers between devices  33.7 us (31%)
  local copies, waits for them, and re-layouts  33 us (30%)
  matrix products  32.8 us (30%)
  other arithmetic  4.2 us (4%)
  between operations  2.76 us (3%)
  waiting for transfers between devices  2.72 us (2%)
    dot_general x48, matrix products, select(): jnp.einsum('...c,cd->...d', values, jnp.asarray(table), precision=exact)  27.5 us
    ppermute x4, starting transfers between devices, with_halo(): before = lax.ppermute(last, axis, up)  14 us
    ppermute x4, starting transfers between devices, with_halo(): after = lax.ppermute(initial, axis, down)  12.4 us
    slice x9, local copies, waits for them, and re-layouts, moved_by(): return jnp.concatenate([empty, values[:, :512 - stride]], axis=1)  7.11 us
    unnamed x213, local copies, waits for them, and re-layouts  6.86 us
    gather x2, local copies, waits for them, and re-layouts, ghost_values(): picked = rows[safe * 4 + opposite]  6.1 us
    dot_general x8, matrix products, ghost_values(): jnp.einsum('bfex,exy->bfy', picked, jnp.asarray(tables[pair]), precision=...  5.34 us
    all_to_all x1, starting transfers between devices, relocate(): lax.all_to_all(places, 'dom', split_axis=1, concat_axis=1, tiled=True)  3.66 us
  transfers between devices with their start and end apart: 10, of which 1 were waited for; matrix products, arithmetic and copies ran while one was open for 39% of the time, Pallas kernels for 0%

commit v1 on v0

v1 whole, which is shorter than its diff:
```python
import functools

import jax
import jax.numpy as jnp
import numpy as np
from jax import lax
from jax.experimental import pallas as pl
from jax.experimental.pallas import tpu as pltpu
from jax.sharding import PartitionSpec as P

MESH = pl.DeviceIdType.MESH
CELLS = 512
CAP = 4
REACH = 16
F32 = jnp.float32
BF16 = jnp.bfloat16


def face_cells(face):
    listed = []
    for first in range(8):
        for second in range(8):
            listed.append(
                (
                    first * 8 + second,
                    448 + first * 8 + second,
                    first * 64 + second,
                    first * 64 + 56 + second,
                    first * 64 + second * 8,
                    first * 64 + second * 8 + 7,
                )[face]
            )
    return listed


def take_table():
    table = np.zeros((CELLS, 384), np.float32)
    for face in range(6):
        for spot, cell in enumerate(face_cells(face)):
            table[cell, face * 64 + spot] = 1.0
    return table


def pool_table():
    table = np.zeros((128, 128), np.float32)
    for half in range(2):
        for a in range(8):
            for b in range(8):
                for u in range(2):
                    for w in range(2):
                        source = (2 * (a % 4) + u) * 8 + 2 * (b % 4) + w
                        table[half * 64 + source, half * 64 + a * 8 + b] = 0.25
    return table


def iota(shape, axis):
    return lax.broadcasted_iota(jnp.int32, shape, axis)


def split(x):
    high = x.astype(BF16)
    return high, (x - high.astype(F32)).astype(BF16)


def dot(a, b):
    return jnp.dot(a, b, preferred_element_type=F32)


def lanes_of(x, index):
    return jnp.take_along_axis(x, index, axis=1, mode="promise_in_bounds")


def adapt_rows(load, store, flags):
    rows = flags.shape[0]
    shape = (rows, 128)
    flag = jnp.broadcast_to(flags, shape)
    octant = jnp.maximum(flag - 1, 0)
    kept = flag == 0
    bx = (octant >> 2) == 1
    by = (octant >> 1) & 1
    bz = octant & 1
    lane = iota(shape, 1)
    y = (lane >> 3) & 7
    z = lane & 7
    half = lane & 64
    low = lane < 64
    ya = 4 * by + (y >> 1)
    za = 4 * bz + (z >> 1)
    yb = jnp.clip(ya + 2 * (y & 1) - 1, 0, 7)
    zb = jnp.clip(za + 2 * (z & 1) - 1, 0, 7)
    index_ya = half + ya * 8 + z
    index_yb = half + yb * 8 + z
    index_za = half + y * 8 + za
    index_zb = half + y * 8 + zb
    index_plain = ya * 8 + za
    v = [load(0, j) for j in range(4)]
    w = [pltpu.roll(chunk, 64, 1) for chunk in v]
    v0 = jnp.where(bx, v[2], v[0])
    v1 = jnp.where(bx, v[3], v[1])
    w0 = jnp.where(bx, w[2], w[0])
    w1 = jnp.where(bx, w[3], w[1])
    before = jnp.where(bx, w[1], v[0])
    after = jnp.where(bx, v[3], w[2])
    near = (
        jnp.where(low, v0, w0),
        jnp.where(low, w0, v0),
        jnp.where(low, v1, w1),
        jnp.where(low, w1, v1),
    )
    far = (
        jnp.where(low, before, v0),
        jnp.where(low, v0, w1),
        jnp.where(low, w0, v1),
        jnp.where(low, v1, after),
    )
    for j in range(4):
        cur = 0.75 * near[j] + 0.25 * far[j]
        cur = 0.75 * lanes_of(cur, index_ya) + 0.25 * lanes_of(cur, index_yb)
        cur = 0.75 * lanes_of(cur, index_za) + 0.25 * lanes_of(cur, index_zb)
        store(0, j, jnp.where(kept, v[j], cur))
    for s in range(1, 4):
        v = [load(s, j) for j in range(4)]
        for j in range(4):
            source = jnp.where(bx, v[2 + j // 2], v[j // 2])
            cur = lanes_of(source, index_plain + (j % 2) * 64)
            store(s, j, jnp.where(kept, v[j], cur))


def kernel(
    peers,
    layers,
    head,
    water_prev,
    alpha,
    shape_n,
    theta_r,
    theta_s,
    sat_cond,
    refine,
    destination,
    neighbours,
    t_take,
    t_put,
    t_pool,
    new_head,
    residual,
    raw,
    sent,
    got,
    work,
    settled,
    got_work,
    place,
    fine_hot,
    pool_hot,
    present,
    faces,
    planes,
    halo,
    ghost_planes,
    fields,
    move_send,
    move_recv,
    halo_send,
    halo_recv,
    plane_send,
    plane_recv,
):
    me = lax.axis_index("dom")
    level = lax.axis_index("depth")
    blocks = head.shape[1]
    both = 2 * blocks
    slots = 8 * peers
    shift = blocks.bit_length() - 1

    halo[...] = jnp.zeros_like(halo)
    ghost_planes[...] = jnp.zeros_like(ghost_planes)
    got[0] = jnp.zeros(got.shape[1:], F32)

    barrier = pltpu.get_barrier_semaphore()
    for k in range(1, peers):
        pl.semaphore_signal(
            barrier, inc=1, device_id=(lax.rem(me + k, peers), level), device_id_type=MESH
        )

    @pl.when(level > 0)
    def _():
        pl.semaphore_signal(barrier, inc=1, device_id=(me, level - 1), device_id_type=MESH)

    @pl.when(level < layers - 1)
    def _():
        pl.semaphore_signal(barrier, inc=1, device_id=(me, level + 1), device_id_type=MESH)

    left = (head, alpha, shape_n, sat_cond)
    right = (water_prev, theta_r, theta_s)
    for s in range(4):
        cols = pl.ds(s * CELLS, CELLS)
        high, rest = split(left[s][0])
        raw[pl.ds(0, blocks), cols] = high
        raw[pl.ds(both, blocks), cols] = rest
        if s < 3:
            high, rest = split(right[s][0])
            raw[pl.ds(blocks, blocks), cols] = high
            raw[pl.ds(both + blocks, blocks), cols] = rest
        else:
            raw[pl.ds(blocks, blocks), cols] = jnp.zeros((blocks, CELLS), BF16)
            raw[pl.ds(both + blocks, blocks), cols] = jnp.zeros((blocks, CELLS), BF16)

    dest = jnp.concatenate([destination[...], destination[...]], axis=1)
    flag_row = jnp.concatenate([refine[...], refine[...]], axis=1)
    owner = dest >> shift
    spot = dest & (blocks - 1)
    shape = (blocks, both)
    own_lane = iota(shape, 1)
    own_row = iota(shape, 0)
    diagonal = own_lane == own_row
    owner_col = jnp.sum(jnp.where(diagonal, owner, 0), axis=1, keepdims=True)
    flag_col = jnp.sum(jnp.where(diagonal, flag_row, 0), axis=1, keepdims=True)
    earlier = (owner_col == owner) & (own_row < (own_lane & (blocks - 1)))
    rank = jnp.sum(earlier.astype(jnp.int32), axis=0, keepdims=True)
    shape = (slots, both)
    row = iota(shape, 0)
    side = (row >> 2) & 1
    target = me + (row >> 3)
    target = jnp.where(target >= peers, target - peers, target)
    chosen = (
        (side == (iota(shape, 1) >> shift))
        & (owner == target)
        & (rank == (row & 3))
        & (row >= 8)
    )
    hot = jnp.where(chosen, 1.0, 0.0)
    spot_sent = jnp.sum(hot * (spot + 1).astype(F32), axis=1, keepdims=True) - 1.0
    flag_sent = jnp.sum(hot * flag_row.astype(F32), axis=1, keepdims=True)
    hot = hot.astype(BF16)
    packed = dot(jnp.concatenate([hot, hot], axis=1), raw[...])
    sent[:, :, pl.ds(0, 4 * CELLS)] = packed.reshape(peers, 8, 4 * CELLS)
    meta = jnp.where(iota((slots, 128), 1) < 64, spot_sent, flag_sent)
    sent[:, :, pl.ds(4 * CELLS, 128)] = meta.reshape(peers, 8, 128)

    @pl.when((level > 0) & (level < layers - 1))
    def _():
        pl.semaphore_wait(barrier, peers + 1)

    @pl.when((level == 0) | (level == layers - 1))
    def _():
        pl.semaphore_wait(barrier, peers)

    moves = []
    for k in range(1, peers):
        moves.append(
            pltpu.make_async_remote_copy(
                src_ref=sent.at[k],
                dst_ref=got.at[k],
                send_sem=move_send.at[k],
                recv_sem=move_recv.at[k],
                device_id=(lax.rem(me + k, peers), level),
                device_id_type=MESH,
            )
        )
    for copy in moves:
        copy.start()

    flags16 = flag_col
    for start in range(0, both, 16):
        base = start % blocks

        def load(s, j, start=start, base=base):
            refs = left if start < blocks else right
            if s == 3 and start >= blocks:
                return jnp.zeros((16, 128), F32)
            return refs[s][0, pl.ds(base, 16), pl.ds(j * 128, 128)]

        def store(s, j, value, start=start):
            cols = pl.ds(s * CELLS + j * 128, 128)
            high, rest = split(value)
            work[pl.ds(start, 16), cols] = high
            work[pl.ds(both + start, 16), cols] = rest

        adapt_rows(load, store, flags16[base : base + 16])
    shape = (both, both)
    wanted = (
        (iota(shape, 0) - spot == ((iota(shape, 0) >> shift) << shift))
        & ((iota(shape, 0) >> shift) == (iota(shape, 1) >> shift))
        & (owner == me)
    )
    hot = jnp.where(wanted, 1.0, 0.0).astype(BF16)
    settled[...] = dot(jnp.concatenate([hot, hot], axis=1), work[...])

    first_row = me * blocks - REACH
    shape = (blocks, 128)
    lane = iota(shape, 1)
    low = lane < 64
    quarter = ((lane >> 5) & 1) * 2 + ((lane >> 2) & 1)
    for chunk in range(2):
        counts = []
        for pair in range(2):
            face = chunk * 2 + pair
            entry = [neighbours[:, pl.ds(face * 4 + e, 1)] for e in range(4)]
            full = entry[3] >= 0
            for e in range(4):
                hot = (lane == entry[e] - first_row) & (entry[e] >= 0)
                rows = pl.ds((pair * 4 + e) * blocks, blocks)
                value = jnp.where(hot & full, 1.0, 0.0).astype(BF16)
                pool_hot[chunk, rows, pl.ds(0, 128)] = value
                pool_hot[chunk, rows, pl.ds(128, 128)] = value
                if e == 0:
                    rows = pl.ds(pair * blocks, blocks)
                    value = jnp.where(hot & jnp.logical_not(full), 1.0, 0.0).astype(BF16)
                    fine_hot[chunk, rows, pl.ds(0, 128)] = value
                    fine_hot[chunk, rows, pl.ds(128, 128)] = value
            counts.append(jnp.where(entry[0] >= 0, 0.5, 0.0))
        present[:, pl.ds(chunk * 128, 128)] = jnp.where(low, counts[0], counts[1])
    low_on = jnp.where(level > 0, 0.5, 0.0)
    high_on = jnp.where(level < layers - 1, 0.5, 0.0)
    present[:, pl.ds(256, 128)] = jnp.where(low, low_on, high_on)
    lift = jnp.where(low, -1.0, 1.0)

    for copy in moves:
        copy.wait()

    meta = got[:, :, pl.ds(4 * CELLS, 128)].reshape(slots, 128)
    spot_got = meta[:, :1]
    flag_got = meta[:, 64:65].astype(jnp.int32)
    shape = (slots, both)
    row = iota(shape, 0)
    used = (
        ((iota(shape, 1) & (blocks - 1)).astype(F32) == spot_got)
        & ((iota(shape, 1) >> shift) == ((row >> 2) & 1))
        & (row >= 8)
    )
    hot = jnp.where(used, 1.0, 0.0).astype(BF16)
    for start in range(0, slots, 16):

        def load(s, j, start=start):
            return got[
                pl.ds(start // 8, 2), :, pl.ds(s * CELLS + j * 128, 128)
            ].reshape(16, 128)

        def store(s, j, value, start=start):
            cols = pl.ds(s * CELLS + j * 128, 128)
            high, rest = split(value)
            got_work[pl.ds(start, 16), cols] = high
            got_work[pl.ds(slots + start, 16), cols] = rest

        adapt_rows(load, store, flag_got[start : start + 16])
    hot = jnp.concatenate([hot, hot], axis=0)
    settled[...] += lax.dot_general(
        hot, got_work[...], (((0,), (0,)), ((), ())), preferred_element_type=F32
    )

    top_rows = pl.ds(0, blocks)
    end_rows = pl.ds(blocks, blocks)
    seg = [pl.ds(s * CELLS, CELLS) for s in range(4)]

    def closure(h):
        n = settled[top_rows, seg[2]]
        m = 1.0 - 1.0 / n
        log_x = jnp.log(settled[top_rows, seg[1]] * jnp.maximum(-h, 0.0))
        log_up = m * jnp.log(1.0 + jnp.exp(n * log_x))
        root = jnp.exp(-0.5 * log_up)
        inner = 1.0 - jnp.exp((n - 1.0) * log_x - log_up)
        resid = settled[end_rows, seg[1]]
        water = resid + (settled[end_rows, seg[2]] - resid) * root * root
        conduct = settled[top_rows, seg[3]] * root * inner * inner
        return water, conduct

    lane_all = iota((blocks, CELLS), 1)

    def evaluate(step, h, diag):
        water, conduct = closure(h)
        terms = jnp.concatenate([*split(h), *split(conduct)], axis=0)
        taken = dot(terms, t_take[...])
        face_h = taken[:blocks] + taken[blocks:both]
        face_k = taken[both : both + blocks] + taken[both + blocks :]
        faces[0] = face_h[:, :256]
        faces[1] = face_k[:, :256]
        edge_h = face_h[:, 256:]
        edge_k = face_k[:, 256:]
        planes[0] = jnp.where(low, edge_h, pltpu.roll(edge_k, 64, 1))
        planes[1] = jnp.where(low, pltpu.roll(edge_h, 64, 1), edge_k)

        def halo_copy(side, way):
            start = 0 if side else blocks - REACH
            return pltpu.make_async_remote_copy(
                src_ref=faces.at[:, pl.ds(start, REACH)],
                dst_ref=halo.at[step, side],
                send_sem=halo_send.at[step, side],
                recv_sem=halo_recv.at[step, side],
                device_id=(me + way, level),
                device_id_type=MESH,
            )

        def plane_copy(side, way):
            return pltpu.make_async_remote_copy(
                src_ref=planes.at[1 - side],
                dst_ref=ghost_planes.at[step, side],
                send_sem=plane_send.at[step, side],
                recv_sem=plane_recv.at[step, side],
                device_id=(me, level + way),
                device_id_type=MESH,
            )

        @pl.when(me < peers - 1)
        def _():
            halo_copy(0, 1).start()

        @pl.when(me > 0)
        def _():
            halo_copy(1, -1).start()

        @pl.when(level < layers - 1)
        def _():
            plane_copy(0, 1).start()

        @pl.when(level > 0)
        def _():
            plane_copy(1, -1).start()

        flux = jnp.zeros((blocks, CELLS), F32)
        total = jnp.zeros((blocks, CELLS), F32)
        for stride, rise in ((64, 0.0), (8, 0.0), (1, 1.0)):
            inside = ((lane_all // stride) & 7) < 7
            near_h = pltpu.roll(h, CELLS - stride, 1)
            near_k = pltpu.roll(conduct, CELLS - stride, 1)
            part = jnp.where(inside, 0.5 * (conduct + near_k), 0.0)
            gain = part * (near_h - h + rise)
            flux = flux + gain - pltpu.roll(gain, stride, 1)
            if diag:
                total = total + part + pltpu.roll(part, stride, 1)
        fields[0] = 4.0 * (water - settled[end_rows, seg[0]]) - flux
        if diag:
            resid = settled[end_rows, seg[1]]
            fields[1] = (
                4.0 * (settled[end_rows, seg[2]] - resid) * settled[top_rows, seg[1]] + total
            )

        @pl.when(me < peers - 1)
        def _():
            halo_copy(0, 1).wait_send()
            halo_copy(1, -1).wait_recv()

        @pl.when(me > 0)
        def _():
            halo_copy(1, -1).wait_send()
            halo_copy(0, 1).wait_recv()

        @pl.when(level < layers - 1)
        def _():
            plane_copy(0, 1).wait_send()
            plane_copy(1, -1).wait_recv()

        @pl.when(level > 0)
        def _():
            plane_copy(1, -1).wait_send()
            plane_copy(0, 1).wait_recv()

        spare = jnp.zeros((128 - blocks - 2 * REACH, 128), F32)
        out_h = []
        out_k = []
        for chunk in range(2):
            cols = pl.ds(chunk * 128, 128)
            terms = []
            for kind in range(2):
                wide = jnp.concatenate(
                    [halo[step, 0, kind, :, cols], faces[kind, :, cols], halo[step, 1, kind, :, cols], spare],
                    axis=0,
                )
                terms.append(jnp.concatenate(split(wide), axis=0))
            pooled = dot(jnp.concatenate(terms, axis=0), t_pool[...])
            pooled = [pooled[:128] + pooled[128:256], pooled[256:384] + pooled[384:]]
            pooled = [jnp.concatenate(split(x), axis=0) for x in pooled]
            fine = dot(fine_hot[chunk], jnp.concatenate(terms, axis=1))
            pool = dot(pool_hot[chunk], jnp.concatenate(pooled, axis=1))
            for kind, out in ((0, out_h), (1, out_k)):
                col = slice(kind * 128, kind * 128 + 128)
                sides = []
                for pair in range(2):
                    quad = [
                        pool[(pair * 4 + e) * blocks : (pair * 4 + e + 1) * blocks, col]
                        for e in range(4)
                    ]
                    hanging = jnp.where(
                        quarter < 2,
                        jnp.where(quarter == 0, quad[0], quad[1]),
                        jnp.where(quarter == 2, quad[2], quad[3]),
                    )
                    sides.append(hanging + fine[pair * blocks : (pair + 1) * blocks, col])
                out.append(pltpu.roll(jnp.where(low, sides[1], sides[0]), 64, 1))
        below = ghost_planes[step, 0]
        above = ghost_planes[step, 1]
        out_h.append(jnp.where(low, below, pltpu.roll(above, 64, 1)) + lift)
        out_k.append(jnp.where(low, pltpu.roll(below, 64, 1), above))
        rim = present[...] * (face_k + jnp.concatenate(out_k, axis=1))
        push = rim * (jnp.concatenate(out_h, axis=1) - face_h)
        if diag:
            spread = dot(jnp.concatenate([*split(push), *split(rim)], axis=0), t_put[...])
            resid = fields[0] - (spread[:blocks] + spread[blocks:both])
            return resid, fields[1] + spread[both : both + blocks] + spread[both + blocks :]
        spread = dot(jnp.concatenate(split(push), axis=0), t_put[...])
        return fields[0] - (spread[:blocks] + spread[blocks:]), None

    start_head = settled[top_rows, seg[0]]
    resid, diag = evaluate(0, start_head, True)
    fresh = start_head - resid / diag
    new_head[0] = fresh
    resid, _ = evaluate(1, fresh, False)
    residual[0] = resid


def on_device(
    peers,
    layers,
    head,
    water_prev,
    alpha,
    shape_n,
    theta_r,
    theta_s,
    sat_cond,
    refine,
    destination,
    neighbours,
):
    blocks = head.shape[1]
    both = 2 * blocks
    slots = 8 * peers
    table = take_table()
    vmem = pl.BlockSpec(memory_space=pltpu.VMEM)
    dma = pltpu.SemaphoreType.DMA
    return pl.pallas_call(
        functools.partial(kernel, peers, layers),
        out_shape=(
            jax.ShapeDtypeStruct(head.shape, F32),
            jax.ShapeDtypeStruct(head.shape, F32),
        ),
        in_specs=[vmem] * 13,
        out_specs=(vmem, vmem),
        scratch_shapes=[
            pltpu.VMEM((2 * both, 4 * CELLS), BF16),
            pltpu.VMEM((peers, 8, 4 * CELLS + 128), F32),
            pltpu.VMEM((peers, 8, 4 * CELLS + 128), F32),
            pltpu.VMEM((2 * both, 4 * CELLS), BF16),
            pltpu.VMEM((both, 4 * CELLS), F32),
            pltpu.VMEM((2 * slots, 4 * CELLS), BF16),
            pltpu.VMEM((8, 128), F32),
            pltpu.VMEM((2, 2 * blocks, 256), BF16),
            pltpu.VMEM((2, 8 * blocks, 256), BF16),
            pltpu.VMEM((blocks, 384), F32),
            pltpu.VMEM((2, blocks, 256), F32),
            pltpu.VMEM((2, blocks, 128), F32),
            pltpu.VMEM((2, 2, 2, REACH, 256), F32),
            pltpu.VMEM((2, 2, blocks, 128), F32),
            pltpu.VMEM((2, blocks, CELLS), F32),
            dma((peers,)),
            dma((peers,)),
            dma((2, 2)),
            dma((2, 2)),
            dma((2, 2)),
            dma((2, 2)),
        ],
        compiler_params=pltpu.CompilerParams(
            collective_id=0, has_side_effects=True, vmem_limit_bytes=48 * 1024 * 1024
        ),
    )(
        head,
        water_prev,
        alpha,
        shape_n,
        theta_r,
        theta_s,
        sat_cond,
        refine.reshape(1, blocks),
        destination.reshape(1, blocks),
        neighbours.reshape(blocks, 16),
        jnp.asarray(table, BF16),
        jnp.asarray(table.T, BF16),
        jnp.asarray(pool_table(), BF16),
    )


def solution(mesh):
    cells = P("depth", "dom", None)
    placed = (cells,) * 7 + (P("dom"), P("dom"), P("dom", None, None))
    return jax.shard_map(
        functools.partial(on_device, mesh.shape["dom"], mesh.shape["depth"]),
        mesh=mesh,
        in_specs=placed,
        out_specs=(cells, cells),
        check_vma=False,
    )
```

time: 110 us -> 31 us (0.28)
  the two profiles are of different devices: /device:TPU:21 before, /device:TPU:0 now
where the time goes in v1:
time: 31 us; the launch traced here: 30.7 us
  Pallas kernels  19.5 us (63%)
  local copies, waits for them, and re-layouts  10.4 us (34%)
  between operations  0.69 us (2%)
    pallas_call x1, Pallas kernels, on_device(): pl.pallas_call(functools.partial(kernel, peers, layers), out_shape=(jax.S...  19.5 us
    unnamed x26, local copies, waits for them, and re-layouts  9.64 us
    reshape x1, local copies, waits for them, and re-layouts, on_device(): neighbours.reshape(blocks, 16)  0.8 us

profile of v1, /device:TPU:0, one launch (start us, length us, event | category | flops | bytes accessed | tf_op | source)
XLA Modules:
  0.0 30.7 jit_solution(13134413923149028605)
XLA Ops:
  0.6 0.0 copy-start.9
  0.6 0.0 copy-start.10
  0.7 0.0 copy-start.11
  0.7 0.8 %copy.16.neighbours = s32[64,16]{1,0:T(8,128)S(1)} copy(s32[64,16]{0,1:T(8,128)} %bitcast.5) | data formatting | bytes 8192 | tf_op jit(solution)/shard_map/reshape | solution.py:575
  1.5 0.0 copy-done.9
  1.5 0.0 copy-done.10
  1.5 0.0 copy-done.11
  1.5 0.0 copy-start
  1.5 1.0 %copy-done = bf16[384,512]{1,0:T(8,128)(2,1)S(1)} copy-done((bf16[384,512]{1,0:T(8,128)(2,1)S(1)}, bf16[384,512]{1,0:T(8,128)(2,1)}, u32[]{:S(2)}) %copy-start) | copy-done | bytes 393240
  2.5 0.0 copy-start.1
  2.5 1.0 %copy-done.1 = bf16[512,384]{1,0:T(8,128)(2,1)S(1)} copy-done((bf16[512,384]{1,0:T(8,128)(2,1)S(1)}, bf16[512,384]{1,0:T(8,128)(2,1)}, u32[]{:S(2)}) %copy-start.1) | copy-done | bytes 393240
  3.5 0.0 copy-start.2
  3.5 0.9 %copy-done.2 = f32[1,64,512]{2,1,0:T(8,128)S(1)} copy-done((f32[1,64,512]{2,1,0:T(8,128)S(1)}, f32[1,64,512]{2,1,0:T(8,128)}, u32[]{:S(2)}) %copy-start.2) | copy-done | bytes 131096
  4.4 0.0 copy-start.3
  4.4 0.9 %copy-done.3 = f32[1,64,512]{2,1,0:T(8,128)S(1)} copy-done((f32[1,64,512]{2,1,0:T(8,128)S(1)}, f32[1,64,512]{2,1,0:T(8,128)}, u32[]{:S(2)}) %copy-start.3) | copy-done | bytes 131096
  5.3 0.0 copy-start.4
  5.3 0.9 %copy-done.4 = f32[1,64,512]{2,1,0:T(8,128)S(1)} copy-done((f32[1,64,512]{2,1,0:T(8,128)S(1)}, f32[1,64,512]{2,1,0:T(8,128)}, u32[]{:S(2)}) %copy-start.4) | copy-done | bytes 131096
  6.2 0.9 %copy-done.5 = f32[1,64,512]{2,1,0:T(8,128)S(1)} copy-done((f32[1,64,512]{2,1,0:T(8,128)S(1)}, f32[1,64,512]{2,1,0:T(8,128)}, u32[]{:S(2)}) %copy-start.5) | copy-done | bytes 131096
  7.1 0.9 %copy-done.6 = f32[1,64,512]{2,1,0:T(8,128)S(1)} copy-done((f32[1,64,512]{2,1,0:T(8,128)S(1)}, f32[1,64,512]{2,1,0:T(8,128)}, u32[]{:S(2)}) %copy-start.6) | copy-done | bytes 131096
  8.0 0.9 %copy-done.7 = f32[1,64,512]{2,1,0:T(8,128)S(1)} copy-done((f32[1,64,512]{2,1,0:T(8,128)S(1)}, f32[1,64,512]{2,1,0:T(8,128)}, u32[]{:S(2)}) %copy-start.7) | copy-done | bytes 131096
  8.9 0.9 %copy-done.8 = f32[1,64,512]{2,1,0:T(8,128)S(1)} copy-done((f32[1,64,512]{2,1,0:T(8,128)S(1)}, f32[1,64,512]{2,1,0:T(8,128)}, u32[]{:S(2)}) %copy-start.8) | copy-done | bytes 131096
  9.8 19.5 %shard_map.140 = (f32[1,64,512]{2,1,0:T(8,128)S(1)}, f32[1,64,512]{2,1,0:T(8,128)S(1)}) custom-call(f32[1,64,512]{2,1,0:T(8,128)S(1)} %copy-done.2, f32[1,64,512]{2,1,0:T(8,128)S(1)} %copy-done.3, f32[1,64,512]{2,1,0:T(8,128)S(1)} %copy-done.4, f32[1,64,512]{2,1,0:T(8,128)S(1)} %copy-done.5, f32[1,64,512]{2,1,0:T(8,128)S(1)} %copy-done.6, ...), custom_call_target="tpu_custom_call" | custom-call | tf_op jit(solution)/shard_map/pallas_call | solution.py:531
  29.3 0.7 %copy.19 = f32[1,64,512]{2,1,0:T(8,128)} copy(f32[1,64,512]{2,1,0:T(8,128)S(1)} %get-tuple-element.4) | data formatting | bytes 262144
  30.0 0.7 %copy.20 = f32[1,64,512]{2,1,0:T(8,128)} copy(f32[1,64,512]{2,1,0:T(8,128)S(1)} %get-tuple-element.5) | data formatting | bytes 262144
  (4 shorter events, 0.0 us)
Async XLA Ops:
  0.6 0.8 %copy-start.9 = (bf16[128,128]{1,0:T(8,128)(2,1)S(1)}, bf16[128,128]{1,0:T(8,128)(2,1)}, u32[]{:S(2)}) copy-start(bf16[128,128]{1,0:T(8,128)(2,1)} %constant.8.clone.t_pool) | copy-start | bytes 98308
  0.6 0.8 %copy-start.10 = (s32[64]{0:T(128)S(1)}, s32[64]{0:T(128)}, u32[]{:S(2)}) copy-start(s32[64]{0:T(128)} %param.20) | copy-start | bytes 772
  0.7 0.8 %copy-start.11 = (s32[64]{0:T(128)S(1)}, s32[64]{0:T(128)}, u32[]{:S(2)}) copy-start(s32[64]{0:T(128)} %param.21) | copy-start | bytes 772
  1.5 1.0 %copy-start = (bf16[384,512]{1,0:T(8,128)(2,1)S(1)}, bf16[384,512]{1,0:T(8,128)(2,1)}, u32[]{:S(2)}) copy-start(bf16[384,512]{1,0:T(8,128)(2,1)} %constant.7.clone.t_put) | copy-start | bytes 1179652
  2.5 1.0 %copy-start.1 = (bf16[512,384]{1,0:T(8,128)(2,1)S(1)}, bf16[512,384]{1,0:T(8,128)(2,1)}, u32[]{:S(2)}) copy-start(bf16[512,384]{1,0:T(8,128)(2,1)} %constant.6.clone.t_take) | copy-start | bytes 1179652
  3.5 0.9 %copy-start.2 = (f32[1,64,512]{2,1,0:T(8,128)S(1)}, f32[1,64,512]{2,1,0:T(8,128)}, u32[]{:S(2)}) copy-start(f32[1,64,512]{2,1,0:T(8,128)} %head.1) | copy-start | bytes 393220
  4.4 0.9 %copy-start.3 = (f32[1,64,512]{2,1,0:T(8,128)S(1)}, f32[1,64,512]{2,1,0:T(8,128)}, u32[]{:S(2)}) copy-start(f32[1,64,512]{2,1,0:T(8,128)} %water_prev.1) | copy-start | bytes 393220
  5.3 0.9 %copy-start.4 = (f32[1,64,512]{2,1,0:T(8,128)S(1)}, f32[1,64,512]{2,1,0:T(8,128)}, u32[]{:S(2)}) copy-start(f32[1,64,512]{2,1,0:T(8,128)} %alpha.1) | copy-start | bytes 393220
  6.2 0.9 %copy-start.5 = (f32[1,64,512]{2,1,0:T(8,128)S(1)}, f32[1,64,512]{2,1,0:T(8,128)}, u32[]{:S(2)}) copy-start(f32[1,64,512]{2,1,0:T(8,128)} %shape_n.1) | copy-start | bytes 393220
  7.1 0.9 %copy-start.6 = (f32[1,64,512]{2,1,0:T(8,128)S(1)}, f32[1,64,512]{2,1,0:T(8,128)}, u32[]{:S(2)}) copy-start(f32[1,64,512]{2,1,0:T(8,128)} %theta_r.1) | copy-start | bytes 393220
  8.0 0.9 %copy-start.7 = (f32[1,64,512]{2,1,0:T(8,128)S(1)}, f32[1,64,512]{2,1,0:T(8,128)}, u32[]{:S(2)}) copy-start(f32[1,64,512]{2,1,0:T(8,128)} %theta_s.1) | copy-start | bytes 393220
  8.9 0.9 %copy-start.8 = (f32[1,64,512]{2,1,0:T(8,128)S(1)}, f32[1,64,512]{2,1,0:T(8,128)}, u32[]{:S(2)}) copy-start(f32[1,64,512]{2,1,0:T(8,128)} %sat_cond.1) | copy-start | bytes 393220

commit v2 on v1

--- a/solution.py
+++ b/solution.py
@@ -129,6 +129,21 @@
 def kernel(
     peers,
     layers,
+    head_hbm,
+    water_prev_hbm,
+    alpha_hbm,
+    shape_n_hbm,
+    theta_r_hbm,
+    theta_s_hbm,
+    sat_cond_hbm,
+    refine_hbm,
+    destination_hbm,
+    neighbours_hbm,
+    t_take_hbm,
+    t_put_hbm,
+    t_pool_hbm,
+    new_head,
+    residual,
     head,
     water_prev,
     alpha,
@@ -142,8 +157,7 @@
     t_take,
     t_put,
     t_pool,
-    new_head,
-    residual,
+    load_sem,
     raw,
     sent,
     got,
@@ -173,6 +187,26 @@
     slots = 8 * peers
     shift = blocks.bit_length() - 1
 
+    loads = []
+    for source, target in (
+        (destination_hbm, destination),
+        (refine_hbm, refine),
+        (head_hbm, head),
+        (water_prev_hbm, water_prev),
+        (alpha_hbm, alpha),
+        (theta_r_hbm, theta_r),
+        (shape_n_hbm, shape_n),
+        (theta_s_hbm, theta_s),
+        (sat_cond_hbm, sat_cond),
+        (neighbours_hbm, neighbours),
+        (t_take_hbm, t_take),
+        (t_pool_hbm, t_pool),
+        (t_put_hbm, t_put),
+    ):
+        loads.append(pltpu.make_async_copy(source, target, load_sem.at[len(loads)]))
+    for copy in loads:
+        copy.start()
+
     halo[...] = jnp.zeros_like(halo)
     ghost_planes[...] = jnp.zeros_like(ghost_planes)
     got[0] = jnp.zeros(got.shape[1:], F32)
@@ -191,6 +225,8 @@
     def _():
         pl.semaphore_signal(barrier, inc=1, device_id=(me, level + 1), device_id_type=MESH)
 
+    for copy in loads[:9]:
+        copy.wait()
     left = (head, alpha, shape_n, sat_cond)
     right = (water_prev, theta_r, theta_s)
     for s in range(4):
@@ -287,7 +323,10 @@
     hot = jnp.where(wanted, 1.0, 0.0).astype(BF16)
     settled[...] = dot(jnp.concatenate([hot, hot], axis=1), work[...])
 
+    for copy in loads[9:]:
+        copy.wait()
     first_row = me * blocks - REACH
+    eye = jnp.where(iota((blocks, blocks), 0) == iota((blocks, blocks), 1), 1.0, 0.0)
     shape = (blocks, 128)
     lane = iota(shape, 1)
     low = lane < 64
@@ -296,7 +335,14 @@
         counts = []
         for pair in range(2):
             face = chunk * 2 + pair
-            entry = [neighbours[:, pl.ds(face * 4 + e, 1)] for e in range(4)]
+            column = lax.dot_general(
+                eye,
+                neighbours[face].astype(F32),
+                (((1,), (1,)), ((), ())),
+                precision=lax.Precision.HIGHEST,
+                preferred_element_type=F32,
+            ).astype(jnp.int32)
+            entry = [column[:, e : e + 1] for e in range(4)]
             full = entry[3] >= 0
             for e in range(4):
                 hot = (lane == entry[e] - first_row) & (entry[e] >= 0)
@@ -527,6 +573,7 @@
     slots = 8 * peers
     table = take_table()
     vmem = pl.BlockSpec(memory_space=pltpu.VMEM)
+    hbm = pl.BlockSpec(memory_space=pltpu.HBM)
     dma = pltpu.SemaphoreType.DMA
     return pl.pallas_call(
         functools.partial(kernel, peers, layers),
@@ -534,9 +581,17 @@
             jax.ShapeDtypeStruct(head.shape, F32),
             jax.ShapeDtypeStruct(head.shape, F32),
         ),
-        in_specs=[vmem] * 13,
+        in_specs=[hbm] * 13,
         out_specs=(vmem, vmem),
-        scratch_shapes=[
+        scratch_shapes=[pltpu.VMEM(head.shape, F32)] * 7
+        + [
+            pltpu.VMEM((1, blocks), jnp.int32),
+            pltpu.VMEM((1, blocks), jnp.int32),
+            pltpu.VMEM((4, 4, blocks), jnp.int32),
+            pltpu.VMEM((CELLS, 384), BF16),
+            pltpu.VMEM((384, CELLS), BF16),
+            pltpu.VMEM((128, 128), BF16),
+            dma((13,)),
             pltpu.VMEM((2 * both, 4 * CELLS), BF16),
             pltpu.VMEM((peers, 8, 4 * CELLS + 128), F32),
             pltpu.VMEM((peers, 8, 4 * CELLS + 128), F32),
@@ -572,7 +627,7 @@
         sat_cond,
         refine.reshape(1, blocks),
         destination.reshape(1, blocks),
-        neighbours.reshape(blocks, 16),
+        neighbours.transpose(1, 2, 0),
         jnp.asarray(table, BF16),
         jnp.asarray(table.T, BF16),
         jnp.asarray(pool_table(), BF16),

time: 31 us -> 34 us (1.097)
  Pallas kernels: 19.5 us -> 21.2 us
  local copies, waits for them, and re-layouts: 10.4 us -> 11.7 us
    unnamed x26 -> x28, local copies, waits for them, and re-layouts: 9.64 us -> 11.7 us
    pallas_call x1, Pallas kernels: 19.5 us -> 21.2 us  [on_device(): pl.pallas_call(functools.partial(kernel, peers, layers), out_shape=(jax.S...]
    reshape x1 -> x0, local copies, waits for them, and re-layouts: 0.8 us -> none  [on_device(): neighbours.reshape(blocks, 16)]
where the time goes in v2:
time: 34 us; the launch traced here: 33.6 us
  Pallas kernels  21.2 us (62%)
  local copies, waits for them, and re-layouts  11.7 us (34%)
  between operations  0.67 us (2%)
    pallas_call x1, Pallas kernels, on_device(): pl.pallas_call(functools.partial(kernel, peers, layers), out_shape=(jax.S...  21.2 us
    unnamed x28, local copies, waits for them, and re-layouts  11.7 us

profile of v2, /device:TPU:0, one launch (start us, length us, event | category | flops | bytes accessed | tf_op | source)
XLA Modules:
  0.0 33.6 jit_solution(4655683533458367535)
XLA Ops:
  0.6 0.0 copy-start.11
  0.6 0.0 copy-start.12
  0.7 0.6 %copy-done.11 = s32[64]{0:T(128)S(1)} copy-done((s32[64]{0:T(128)S(1)}, s32[64]{0:T(128)}, u32[]{:S(2)}) %copy-start.11) | copy-done | bytes 280
  1.3 0.0 copy-done.12
  1.3 0.0 copy-start
  1.3 1.0 %copy-done = bf16[384,512]{1,0:T(8,128)(2,1)S(1)} copy-done((bf16[384,512]{1,0:T(8,128)(2,1)S(1)}, bf16[384,512]{1,0:T(8,128)(2,1)}, u32[]{:S(2)}) %copy-start) | copy-done | bytes 393240
  2.3 1.0 %copy-done.1 = bf16[512,384]{1,0:T(8,128)(2,1)S(1)} copy-done((bf16[512,384]{1,0:T(8,128)(2,1)S(1)}, bf16[512,384]{1,0:T(8,128)(2,1)}, u32[]{:S(2)}) %copy-start.1) | copy-done | bytes 393240
  3.3 0.0 copy-start.2
  3.3 0.9 %copy-done.2 = f32[1,64,512]{2,1,0:T(8,128)S(1)} copy-done((f32[1,64,512]{2,1,0:T(8,128)S(1)}, f32[1,64,512]{2,1,0:T(8,128)}, u32[]{:S(2)}) %copy-start.2) | copy-done | bytes 131096
  4.2 0.0 copy-start.3
  4.2 0.9 %copy-done.3 = f32[1,64,512]{2,1,0:T(8,128)S(1)} copy-done((f32[1,64,512]{2,1,0:T(8,128)S(1)}, f32[1,64,512]{2,1,0:T(8,128)}, u32[]{:S(2)}) %copy-start.3) | copy-done | bytes 131096
  5.1 0.0 copy-start.4
  5.1 0.9 %copy-done.4 = f32[1,64,512]{2,1,0:T(8,128)S(1)} copy-done((f32[1,64,512]{2,1,0:T(8,128)S(1)}, f32[1,64,512]{2,1,0:T(8,128)}, u32[]{:S(2)}) %copy-start.4) | copy-done | bytes 131096
  6.0 0.0 copy-start.5
  6.0 0.9 %copy-done.5 = f32[1,64,512]{2,1,0:T(8,128)S(1)} copy-done((f32[1,64,512]{2,1,0:T(8,128)S(1)}, f32[1,64,512]{2,1,0:T(8,128)}, u32[]{:S(2)}) %copy-start.5) | copy-done | bytes 131096
  6.9 0.0 copy-start.6
  6.9 0.9 %copy-done.6 = f32[1,64,512]{2,1,0:T(8,128)S(1)} copy-done((f32[1,64,512]{2,1,0:T(8,128)S(1)}, f32[1,64,512]{2,1,0:T(8,128)}, u32[]{:S(2)}) %copy-start.6) | copy-done | bytes 131096
  7.8 0.9 %copy-done.7 = f32[1,64,512]{2,1,0:T(8,128)S(1)} copy-done((f32[1,64,512]{2,1,0:T(8,128)S(1)}, f32[1,64,512]{2,1,0:T(8,128)}, u32[]{:S(2)}) %copy-start.7) | copy-done | bytes 131096
  8.7 0.9 %copy-done.8 = f32[1,64,512]{2,1,0:T(8,128)S(1)} copy-done((f32[1,64,512]{2,1,0:T(8,128)S(1)}, f32[1,64,512]{2,1,0:T(8,128)}, u32[]{:S(2)}) %copy-start.8) | copy-done | bytes 131096
  9.6 0.8 %copy-done.9 = bf16[128,128]{1,0:T(8,128)(2,1)S(1)} copy-done((bf16[128,128]{1,0:T(8,128)(2,1)S(1)}, bf16[128,128]{1,0:T(8,128)(2,1)}, u32[]{:S(2)}) %copy-start.9) | copy-done | bytes 32792
  10.4 0.7 %copy-done.10 = s32[64,4,4]{0,2,1:T(4,128)S(1)} copy-done((s32[64,4,4]{0,2,1:T(4,128)S(1)}, s32[64,4,4]{0,2,1:T(4,128)}, u32[]{:S(2)}) %copy-start.10) | copy-done | bytes 4120
  11.1 21.2 %shard_map.140 = (f32[1,64,512]{2,1,0:T(8,128)S(1)}, f32[1,64,512]{2,1,0:T(8,128)S(1)}) custom-call(f32[1,64,512]{2,1,0:T(8,128)S(1)} %copy-done.2, f32[1,64,512]{2,1,0:T(8,128)S(1)} %copy-done.3, f32[1,64,512]{2,1,0:T(8,128)S(1)} %copy-done.4, f32[1,64,512]{2,1,0:T(8,128)S(1)} %copy-done.5, f32[1,64,512]{2,1,0:T(8,128)S(1)} %copy-done.6, ...), custom_call_target="tpu_custom_call" | custom-call | tf_op jit(solution)/shard_map/pallas_call | solution.py:578
  32.3 0.7 %copy.17 = f32[1,64,512]{2,1,0:T(8,128)} copy(f32[1,64,512]{2,1,0:T(8,128)S(1)} %get-tuple-element.4) | data formatting | bytes 262144
  32.9 0.7 %copy.18 = f32[1,64,512]{2,1,0:T(8,128)} copy(f32[1,64,512]{2,1,0:T(8,128)S(1)} %get-tuple-element.5) | data formatting | bytes 262144
  (5 shorter events, 0.0 us)
Async XLA Ops:
  0.6 0.7 %copy-start.11 = (s32[64]{0:T(128)S(1)}, s32[64]{0:T(128)}, u32[]{:S(2)}) copy-start(s32[64]{0:T(128)} %param.20) | copy-start | bytes 772
  0.6 0.7 %copy-start.12 = (s32[64]{0:T(128)S(1)}, s32[64]{0:T(128)}, u32[]{:S(2)}) copy-start(s32[64]{0:T(128)} %param.21) | copy-start | bytes 772
  1.3 1.0 %copy-start = (bf16[384,512]{1,0:T(8,128)(2,1)S(1)}, bf16[384,512]{1,0:T(8,128)(2,1)}, u32[]{:S(2)}) copy-start(bf16[384,512]{1,0:T(8,128)(2,1)} %constant.7.clone.t_put_hbm) | copy-start | bytes 1179652
  2.3 1.0 %copy-start.1 = (bf16[512,384]{1,0:T(8,128)(2,1)S(1)}, bf16[512,384]{1,0:T(8,128)(2,1)}, u32[]{:S(2)}) copy-start(bf16[512,384]{1,0:T(8,128)(2,1)} %constant.6.clone.t_take_hbm) | copy-start | bytes 1179652
  3.3 0.9 %copy-start.2 = (f32[1,64,512]{2,1,0:T(8,128)S(1)}, f32[1,64,512]{2,1,0:T(8,128)}, u32[]{:S(2)}) copy-start(f32[1,64,512]{2,1,0:T(8,128)} %head_hbm.1) | copy-start | bytes 393220
  4.2 0.9 %copy-start.3 = (f32[1,64,512]{2,1,0:T(8,128)S(1)}, f32[1,64,512]{2,1,0:T(8,128)}, u32[]{:S(2)}) copy-start(f32[1,64,512]{2,1,0:T(8,128)} %water_prev_hbm.1) | copy-start | bytes 393220
  5.1 0.9 %copy-start.4 = (f32[1,64,512]{2,1,0:T(8,128)S(1)}, f32[1,64,512]{2,1,0:T(8,128)}, u32[]{:S(2)}) copy-start(f32[1,64,512]{2,1,0:T(8,128)} %alpha_hbm.1) | copy-start | bytes 393220
  6.0 0.9 %copy-start.5 = (f32[1,64,512]{2,1,0:T(8,128)S(1)}, f32[1,64,512]{2,1,0:T(8,128)}, u32[]{:S(2)}) copy-start(f32[1,64,512]{2,1,0:T(8,128)} %shape_n_hbm.1) | copy-start | bytes 393220
  6.9 0.9 %copy-start.6 = (f32[1,64,512]{2,1,0:T(8,128)S(1)}, f32[1,64,512]{2,1,0:T(8,128)}, u32[]{:S(2)}) copy-start(f32[1,64,512]{2,1,0:T(8,128)} %theta_r_hbm.1) | copy-start | bytes 393220
  7.8 0.9 %copy-start.7 = (f32[1,64,512]{2,1,0:T(8,128)S(1)}, f32[1,64,512]{2,1,0:T(8,128)}, u32[]{:S(2)}) copy-start(f32[1,64,512]{2,1,0:T(8,128)} %theta_s_hbm.1) | copy-start | bytes 393220
  8.7 0.9 %copy-start.8 = (f32[1,64,512]{2,1,0:T(8,128)S(1)}, f32[1,64,512]{2,1,0:T(8,128)}, u32[]{:S(2)}) copy-start(f32[1,64,512]{2,1,0:T(8,128)} %sat_cond_hbm.1) | copy-start | bytes 393220
  9.6 0.8 %copy-start.9 = (bf16[128,128]{1,0:T(8,128)(2,1)S(1)}, bf16[128,128]{1,0:T(8,128)(2,1)}, u32[]{:S(2)}) copy-start(bf16[128,128]{1,0:T(8,128)(2,1)} %constant.8.clone.t_pool_hbm) | copy-start | bytes 98308
  10.4 0.7 %copy-start.10 = (s32[64,4,4]{0,2,1:T(4,128)S(1)}, s32[64,4,4]{0,2,1:T(4,128)}, u32[]{:S(2)}) copy-start(s32[64,4,4]{0,2,1:T(4,128)} %param.22) | copy-start | bytes 12292

commit v3 on v2

--- a/solution.py
+++ b/solution.py
@@ -615,7 +615,7 @@
             dma((2, 2)),
         ],
         compiler_params=pltpu.CompilerParams(
-            collective_id=0, has_side_effects=True, vmem_limit_bytes=48 * 1024 * 1024
+            collective_id=0, has_side_effects=True, vmem_limit_bytes=60 * 1024 * 1024
         ),
     )(
         head,

time: 34 us -> 23.4 us (0.69)
  local copies, waits for them, and re-layouts: 11.7 us -> 2.26 us
  Pallas kernels: 21.2 us -> 20.3 us
    unnamed x28 -> x4, local copies, waits for them, and re-layouts: 11.7 us -> 2.26 us
    pallas_call x1, Pallas kernels: 21.2 us -> 20.3 us  [on_device(): pl.pallas_call(functools.partial(kernel, peers, layers), out_shape=(jax.S...]
where the time goes in v3:
time: 23.4 us; the launch traced here: 23.2 us
  Pallas kernels  20.3 us (87%)
  local copies, waits for them, and re-layouts  2.26 us (10%)
  between operations  0.65 us (3%)
    pallas_call x1, Pallas kernels, on_device(): pl.pallas_call(functools.partial(kernel, peers, layers), out_shape=(jax.S...  20.3 us
    unnamed x4, local copies, waits for them, and re-layouts  2.26 us

profile of v3, /device:TPU:0, one launch (start us, length us, event | category | flops | bytes accessed | tf_op | source)
XLA Modules:
  0.0 23.2 jit_solution(14278488796170556718)
XLA Ops:
  0.6 20.3 %shard_map.140 = (f32[1,64,512]{2,1,0:T(8,128)}, f32[1,64,512]{2,1,0:T(8,128)}) custom-call(f32[1,64,512]{2,1,0:T(8,128)} %head_hbm.1, f32[1,64,512]{2,1,0:T(8,128)} %water_prev_hbm.1, f32[1,64,512]{2,1,0:T(8,128)} %alpha_hbm.1, f32[1,64,512]{2,1,0:T(8,128)} %shape_n_hbm.1, f32[1,64,512]{2,1,0:T(8,128)} %theta_r_hbm.1, f32[1,64,512]{2,1,0:T(8,128)} %theta_s_hbm.1, ...), custom_call_target="tpu_custom_call" | custom-call | tf_op jit(solution)/shard_map/pallas_call | solution.py:578
  20.9 0.0 copy-start
  21.0 1.6 %copy.17 = f32[1,64,512]{2,1,0:T(8,128)} copy(f32[1,64,512]{2,1,0:T(8,128)} %get-tuple-element.4) | data formatting | bytes 262144
  22.6 0.0 copy-done
  22.6 0.7 %copy.18 = f32[1,64,512]{2,1,0:T(8,128)} copy(f32[1,64,512]{2,1,0:T(8,128)S(1)} %copy-done) | data formatting | bytes 262144
Async XLA Ops:
  20.9 1.6 %copy-start = (f32[1,64,512]{2,1,0:T(8,128)S(1)}, f32[1,64,512]{2,1,0:T(8,128)}, u32[]{:S(2)}) copy-start(f32[1,64,512]{2,1,0:T(8,128)} %get-tuple-element.5) | copy-start | bytes 393220

commit v4 on v3

v4 whole, which is shorter than its diff:
```python
import functools

import jax
import jax.numpy as jnp
import numpy as np
from jax import lax
from jax.experimental import pallas as pl
from jax.experimental.pallas import tpu as pltpu
from jax.sharding import PartitionSpec as P

MESH = pl.DeviceIdType.MESH
CELLS = 512
CAP = 4
REACH = 16
F32 = jnp.float32
BF16 = jnp.bfloat16


def face_cells(face):
    listed = []
    for first in range(8):
        for second in range(8):
            listed.append(
                (
                    first * 8 + second,
                    448 + first * 8 + second,
                    first * 64 + second,
                    first * 64 + 56 + second,
                    first * 64 + second * 8,
                    first * 64 + second * 8 + 7,
                )[face]
            )
    return listed


def take_table():
    table = np.zeros((CELLS, 384), np.float32)
    for face in range(6):
        for spot, cell in enumerate(face_cells(face)):
            table[cell, face * 64 + spot] = 1.0
    return table


def pool_table():
    table = np.zeros((128, 128), np.float32)
    for half in range(2):
        for a in range(8):
            for b in range(8):
                for u in range(2):
                    for w in range(2):
                        source = (2 * (a % 4) + u) * 8 + 2 * (b % 4) + w
                        table[half * 64 + source, half * 64 + a * 8 + b] = 0.25
    return table


def iota(shape, axis):
    return lax.broadcasted_iota(jnp.int32, shape, axis)


def split(x):
    high = x.astype(BF16)
    return high, (x - high.astype(F32)).astype(BF16)


def dot(a, b):
    return jnp.dot(a, b, preferred_element_type=F32)


def lanes_of(x, index):
    return jnp.take_along_axis(x, index, axis=1, mode="promise_in_bounds")


def adapt_rows(load, flags, plain):
    made = {}

    def store(s, j, value):
        made[s, j] = value

    rows = flags.shape[0]
    shape = (rows, 128)
    flag = jnp.broadcast_to(flags, shape)
    octant = jnp.maximum(flag - 1, 0)
    kept = flag == 0
    bx = (octant >> 2) == 1
    by = (octant >> 1) & 1
    bz = octant & 1
    lane = iota(shape, 1)
    y = (lane >> 3) & 7
    z = lane & 7
    half = lane & 64
    low = lane < 64
    ya = 4 * by + (y >> 1)
    za = 4 * bz + (z >> 1)
    yb = jnp.clip(ya + 2 * (y & 1) - 1, 0, 7)
    zb = jnp.clip(za + 2 * (z & 1) - 1, 0, 7)
    index_ya = half + ya * 8 + z
    index_yb = half + yb * 8 + z
    index_za = half + y * 8 + za
    index_zb = half + y * 8 + zb
    index_plain = ya * 8 + za
    v = [load(0, j) for j in range(4)]
    w = [pltpu.roll(chunk, 64, 1) for chunk in v]
    v0 = jnp.where(bx, v[2], v[0])
    v1 = jnp.where(bx, v[3], v[1])
    w0 = jnp.where(bx, w[2], w[0])
    w1 = jnp.where(bx, w[3], w[1])
    before = jnp.where(bx, w[1], v[0])
    after = jnp.where(bx, v[3], w[2])
    near = (
        jnp.where(low, v0, w0),
        jnp.where(low, w0, v0),
        jnp.where(low, v1, w1),
        jnp.where(low, w1, v1),
    )
    far = (
        jnp.where(low, before, v0),
        jnp.where(low, v0, w1),
        jnp.where(low, w0, v1),
        jnp.where(low, v1, after),
    )
    for j in range(4):
        cur = 0.75 * near[j] + 0.25 * far[j]
        cur = 0.75 * lanes_of(cur, index_ya) + 0.25 * lanes_of(cur, index_yb)
        cur = 0.75 * lanes_of(cur, index_za) + 0.25 * lanes_of(cur, index_zb)
        store(0, j, jnp.where(kept, v[j], cur))
    for s in range(1, plain + 1):
        v = [load(s, j) for j in range(4)]
        for j in range(4):
            source = jnp.where(bx, v[2 + j // 2], v[j // 2])
            cur = lanes_of(source, index_plain + (j % 2) * 64)
            store(s, j, jnp.where(kept, v[j], cur))
    return made


def closure(h, alpha, n, cond):
    m = 1.0 - 1.0 / n
    log_x = jnp.log(alpha * jnp.maximum(-h, 0.0))
    log_up = m * jnp.log(1.0 + jnp.exp(n * log_x))
    root = jnp.exp(-0.5 * log_up)
    if cond is None:
        return root, None
    inner = 1.0 - jnp.exp((n - 1.0) * log_x - log_up)
    return root, cond * root * inner * inner


def kernel(
    peers,
    layers,
    head_hbm,
    water_prev_hbm,
    alpha_hbm,
    shape_n_hbm,
    theta_r_hbm,
    theta_s_hbm,
    sat_cond_hbm,
    refine_hbm,
    destination_hbm,
    neighbours_hbm,
    t_take_hbm,
    t_put_hbm,
    t_pool_hbm,
    new_head,
    residual,
    head,
    water_prev,
    alpha,
    shape_n,
    theta_r,
    theta_s,
    sat_cond,
    refine,
    destination,
    neighbours,
    t_take,
    t_put,
    t_pool,
    load_sem,
    raw,
    sent_a,
    sent_b,
    got_a,
    got_b,
    work_a,
    work_b,
    place,
    settled_a,
    settled_b,
    own_hot,
    halo_hot,
    present,
    faces,
    ghosts,
    halo,
    ghost_planes,
    a_send,
    a_recv,
    b_send,
    b_recv,
    halo_send,
    halo_recv,
    plane_send,
    plane_recv,
):
    me = lax.axis_index("dom")
    level = lax.axis_index("depth")
    blocks = head.shape[1]
    both = 2 * blocks
    slots = 8 * peers
    shift = blocks.bit_length() - 1

    loads = []
    for source, target in (
        (destination_hbm, destination),
        (refine_hbm, refine),
        (head_hbm, head),
        (water_prev_hbm, water_prev),
        (alpha_hbm, alpha),
        (theta_r_hbm, theta_r),
        (shape_n_hbm, shape_n),
        (theta_s_hbm, theta_s),
        (sat_cond_hbm, sat_cond),
        (neighbours_hbm, neighbours),
        (t_take_hbm, t_take),
        (t_pool_hbm, t_pool),
        (t_put_hbm, t_put),
    ):
        loads.append(pltpu.make_async_copy(source, target, load_sem.at[len(loads)]))
    for copy in loads:
        copy.start()

    halo[...] = jnp.zeros_like(halo)
    ghost_planes[...] = jnp.zeros_like(ghost_planes)
    got_a[0] = jnp.zeros(got_a.shape[1:], F32)
    got_b[0] = jnp.zeros(got_b.shape[1:], F32)

    barrier = pltpu.get_barrier_semaphore()
    for k in range(1, peers):
        pl.semaphore_signal(
            barrier, inc=1, device_id=(lax.rem(me + k, peers), level), device_id_type=MESH
        )

    @pl.when(level > 0)
    def _():
        pl.semaphore_signal(barrier, inc=1, device_id=(me, level - 1), device_id_type=MESH)

    @pl.when(level < layers - 1)
    def _():
        pl.semaphore_signal(barrier, inc=1, device_id=(me, level + 1), device_id_type=MESH)

    for copy in loads[:9]:
        copy.wait()
    left = (head, alpha, shape_n, sat_cond)
    right = (water_prev, theta_r, theta_s)
    for s in range(4):
        cols = pl.ds(s * CELLS, CELLS)
        high, rest = split(left[s][0])
        raw[pl.ds(0, blocks), cols] = high
        raw[pl.ds(both, blocks), cols] = rest
        if s < 3:
            high, rest = split(right[s][0])
            raw[pl.ds(blocks, blocks), cols] = high
            raw[pl.ds(both + blocks, blocks), cols] = rest
        else:
            raw[pl.ds(blocks, blocks), cols] = jnp.zeros((blocks, CELLS), BF16)
            raw[pl.ds(both + blocks, blocks), cols] = jnp.zeros((blocks, CELLS), BF16)

    dest = jnp.concatenate([destination[...], destination[...]], axis=1)
    flag_row = jnp.concatenate([refine[...], refine[...]], axis=1)
    owner = dest >> shift
    spot = dest & (blocks - 1)
    shape = (blocks, both)
    own_lane = iota(shape, 1)
    own_row = iota(shape, 0)
    diagonal = own_lane == own_row
    owner_col = jnp.sum(jnp.where(diagonal, owner, 0), axis=1, keepdims=True)
    flag_col = jnp.sum(jnp.where(diagonal, flag_row, 0), axis=1, keepdims=True)
    earlier = (owner_col == owner) & (own_row < (own_lane & (blocks - 1)))
    rank = jnp.sum(earlier.astype(jnp.int32), axis=0, keepdims=True)
    shape = (slots, both)
    row = iota(shape, 0)
    side = (row >> 2) & 1
    target = me + (row >> 3)
    target = jnp.where(target >= peers, target - peers, target)
    chosen = (
        (side == (iota(shape, 1) >> shift))
        & (owner == target)
        & (rank == (row & 3))
        & (row >= 8)
    )
    hot = jnp.where(chosen, 1.0, 0.0)
    spot_sent = jnp.sum(hot * (spot + 1).astype(F32), axis=1, keepdims=True) - 1.0
    flag_sent = jnp.sum(hot * flag_row.astype(F32), axis=1, keepdims=True)
    hot = hot.astype(BF16)
    packed = dot(jnp.concatenate([hot, hot], axis=1), raw[...])
    filled = spot_sent >= 0.0
    for start in range(0, slots, 16):
        rows = slice(start, start + 16)
        made = adapt_rows(
            lambda s, j: packed[rows, s * CELLS + j * 128 : s * CELLS + (j + 1) * 128],
            flag_sent[rows].astype(jnp.int32),
            3,
        )
        upper = (iota((16, 128), 0) & 4) == 0
        peer = pl.ds(start // 8, 2)
        for j in range(4):
            conduct = closure(made[0, j], made[1, j], made[2, j], made[3, j])[1]
            conduct = jnp.where(filled[rows], conduct, 0.0)
            pair = jnp.where(upper, made[0, j], pltpu.roll(conduct, 4, 0))
            sent_a[peer, :, pl.ds(j * 128, 128)] = pair.reshape(2, 8, 128)
            for s, value in (
                (0, made[1, j]),
                (1, made[2, j]),
                (2, jnp.where(upper, made[3, j], made[0, j])),
            ):
                cols = pl.ds(s * CELLS + j * 128, 128)
                sent_b[peer, :, cols] = value.reshape(2, 8, 128)
        meta = jnp.broadcast_to(spot_sent[rows], (16, 128))
        sent_a[peer, :, pl.ds(CELLS, 128)] = meta.reshape(2, 8, 128)

    @pl.when((level > 0) & (level < layers - 1))
    def _():
        pl.semaphore_wait(barrier, peers + 1)

    @pl.when((level == 0) | (level == layers - 1))
    def _():
        pl.semaphore_wait(barrier, peers)

    moves_a = []
    moves_b = []
    for moves, source, target, gone, come in (
        (moves_a, sent_a, got_a, a_send, a_recv),
        (moves_b, sent_b, got_b, b_send, b_recv),
    ):
        for k in range(1, peers):
            moves.append(
                pltpu.make_async_remote_copy(
                    src_ref=source.at[k],
                    dst_ref=target.at[k],
                    send_sem=gone.at[k],
                    recv_sem=come.at[k],
                    device_id=(lax.rem(me + k, peers), level),
                    device_id_type=MESH,
                )
            )
    for copy in moves_a + moves_b:
        copy.start()

    def put_rows(work, start, cols, value):
        high, rest = split(value)
        work[pl.ds(start, 16), cols] = high
        work[pl.ds(both + start, 16), cols] = rest

    for start in range(0, blocks, 16):
        made = adapt_rows(
            lambda s, j: left[s][0, pl.ds(start, 16), pl.ds(j * 128, 128)],
            flag_col[start : start + 16],
            3,
        )
        for j in range(4):
            conduct = closure(made[0, j], made[1, j], made[2, j], made[3, j])[1]
            put_rows(work_a, start, pl.ds(j * 128, 128), made[0, j])
            put_rows(work_a, blocks + start, pl.ds(j * 128, 128), conduct)
            for s in range(3):
                put_rows(work_b, start, pl.ds(s * CELLS + j * 128, 128), made[s + 1, j])
    shape = (both, both)
    wanted = (
        ((iota(shape, 0) & (blocks - 1)) == spot)
        & ((iota(shape, 0) >> shift) == (iota(shape, 1) >> shift))
        & (owner == me)
    )
    hot = jnp.where(wanted, 1.0, 0.0).astype(BF16)
    place[...] = jnp.concatenate([hot, hot], axis=1)
    settled_a[...] = dot(place[...], work_a[...])

    for copy in loads[9:]:
        copy.wait()
    eye = jnp.where(iota((blocks, blocks), 0) == iota((blocks, blocks), 1), 1.0, 0.0)
    shape = (blocks, 128)
    lane = iota(shape, 1)
    low = lane < 64
    for face in range(4):
        column = lax.dot_general(
            eye,
            neighbours[face].astype(F32),
            (((1,), (1,)), ((), ())),
            precision=lax.Precision.HIGHEST,
            preferred_element_type=F32,
        ).astype(jnp.int32)
        entry = [jnp.broadcast_to(column[:, e : e + 1], shape) for e in range(4)]
        full = entry[3] >= 0
        present[face] = jnp.where(entry[0] >= 0, 0.5, 0.0)
        wants = [jnp.where(full, -1, entry[0])] + [jnp.where(full, entry[e], -1) for e in range(4)]
        outer = []
        for number, want in enumerate(wants):
            gap = want - me * blocks
            listed = want >= 0
            hit = ((lane & (blocks - 1)) == gap) & listed
            own_hot[face, :, pl.ds(number * 128, 128)] = jnp.where(hit, 1.0, 0.0).astype(BF16)
            spot_out = jnp.where(gap < 0, gap + REACH, gap - blocks + REACH)
            hit = ((lane & (2 * REACH - 1)) == spot_out) & listed & ((gap < 0) | (gap >= blocks))
            outer.append(jnp.where(hit, 1.0, 0.0))
        outer.append(jnp.zeros(shape, F32))
        for number in range(3):
            value = jnp.where(low, outer[2 * number], outer[2 * number + 1])
            halo_hot[face, :, pl.ds(number * 128, 128)] = value.astype(BF16)
    low_on = jnp.where(level > 0, 0.5, 0.0)
    high_on = jnp.where(level < layers - 1, 0.5, 0.0)
    lane_q = iota((128, 128), 1)
    quarter = ((lane_q >> 5) & 1) * 2 + ((lane_q >> 2) & 1)
    masks = [jnp.where(quarter == e, 1.0, 0.0).astype(BF16) for e in range(4)]

    for copy in moves_a:
        copy.wait_recv()
    spot_got = got_a[:, :, pl.ds(CELLS, 128)].reshape(slots, 128)
    shape = (slots, both)
    row = iota(shape, 0)
    used = (
        ((iota(shape, 1) & (blocks - 1)).astype(F32) == spot_got)
        & ((iota(shape, 1) >> shift) == ((row >> 2) & 1))
        & (row >= 8)
    )
    hot = jnp.where(used, 1.0, 0.0).astype(BF16)
    used_hot = jnp.concatenate([hot, hot], axis=0)

    def scatter(value):
        return lax.dot_general(
            used_hot,
            jnp.concatenate(split(value), axis=0),
            (((0,), (0,)), ((), ())),
            preferred_element_type=F32,
        )

    settled_a[...] += scatter(got_a[:, :, pl.ds(0, CELLS)].reshape(slots, CELLS))

    top_rows = pl.ds(0, blocks)
    end_rows = pl.ds(blocks, blocks)
    seg = [pl.ds(s * CELLS, CELLS) for s in range(3)]
    lane_all = iota((blocks, CELLS), 1)

    def other_fields():
        for start in range(0, blocks, 16):
            made = adapt_rows(
                lambda s, j: right[s][0, pl.ds(start, 16), pl.ds(j * 128, 128)],
                flag_col[start : start + 16],
                2,
            )
            for j in range(4):
                for s, value in ((0, made[1, j]), (1, made[2, j]), (2, made[0, j])):
                    put_rows(work_b, blocks + start, pl.ds(s * CELLS + j * 128, 128), value)
        settled_b[...] = dot(place[...], work_b[...])
        for copy in moves_b:
            copy.wait_recv()
        settled_b[...] += scatter(got_b[...].reshape(slots, 3 * CELLS))

    def water_of(root):
        resid = settled_b[end_rows, seg[0]]
        return resid + (settled_b[end_rows, seg[1]] - resid) * root * root

    def gather_table(high, rest, pooled_high, pooled_rest):
        parts = [high, rest]
        for mask in masks:
            parts += [pooled_high * mask[: high.shape[0]], pooled_rest * mask[: high.shape[0]]]
        return parts

    def pool(stacked):
        high, rest = split(stacked)
        both_parts = dot(jnp.concatenate([high, rest], axis=0), t_pool[...])
        count = stacked.shape[0]
        pooled_high, pooled_rest = split(both_parts[:count] + both_parts[count:])
        return high, rest, pooled_high, pooled_rest

    opposite = (1, 0, 3, 2)

    def evaluate(step, h, conduct, meanwhile):
        terms = jnp.concatenate([*split(h), *split(conduct)], axis=0)
        taken = dot(terms, t_take[...])
        face_h = taken[:blocks] + taken[blocks:both]
        face_k = taken[both : both + blocks] + taken[both + blocks :]
        for chunk in range(3):
            part_h = face_h[:, chunk * 128 : chunk * 128 + 128]
            part_k = face_k[:, chunk * 128 : chunk * 128 + 128]
            faces[2 * chunk] = jnp.where(low, part_h, pltpu.roll(part_k, 64, 1))
            faces[2 * chunk + 1] = jnp.where(low, pltpu.roll(part_h, 64, 1), part_k)

        def halo_copy(side, way):
            start = 0 if side else blocks - REACH
            return pltpu.make_async_remote_copy(
                src_ref=faces.at[pl.ds(0, 4), pl.ds(start, REACH)],
                dst_ref=halo.at[step, side],
                send_sem=halo_send.at[step, side],
                recv_sem=halo_recv.at[step, side],
                device_id=(me + way, level),
                device_id_type=MESH,
            )

        def plane_copy(side, way):
            return pltpu.make_async_remote_copy(
                src_ref=faces.at[5 - side],
                dst_ref=ghost_planes.at[step, side],
                send_sem=plane_send.at[step, side],
                recv_sem=plane_recv.at[step, side],
                device_id=(me, level + way),
                device_id_type=MESH,
            )

        @pl.when(me < peers - 1)
        def _():
            halo_copy(0, 1).start()

        @pl.when(me > 0)
        def _():
            halo_copy(1, -1).start()

        @pl.when(level < layers - 1)
        def _():
            plane_copy(0, 1).start()

        @pl.when(level > 0)
        def _():
            plane_copy(1, -1).start()

        flux = jnp.zeros((blocks, CELLS), F32)
        total = jnp.zeros((blocks, CELLS), F32)
        for stride, rise in ((64, 0.0), (8, 0.0), (1, 1.0)):
            inside = (lane_all & (7 * stride)) < 7 * stride
            near_h = pltpu.roll(h, CELLS - stride, 1)
            near_k = pltpu.roll(conduct, CELLS - stride, 1)
            part = jnp.where(inside, 0.5 * (conduct + near_k), 0.0)
            gain = part * (near_h - h + rise)
            flux = flux + gain - pltpu.roll(gain, stride, 1)
            if step == 0:
                total = total + part + pltpu.roll(part, stride, 1)
        parts = pool(faces[pl.ds(0, 4)].reshape(4 * blocks, 128))
        for face in range(4):
            rows = slice(opposite[face] * blocks, (opposite[face] + 1) * blocks)
            table = gather_table(*[part[rows] for part in parts])
            ghosts[face] = dot(own_hot[face], jnp.concatenate(table, axis=0))
        resid, diag = meanwhile(flux, total)

        @pl.when(me < peers - 1)
        def _():
            halo_copy(0, 1).wait_send()
            halo_copy(1, -1).wait_recv()

        @pl.when(me > 0)
        def _():
            halo_copy(1, -1).wait_send()
            halo_copy(0, 1).wait_recv()

        @pl.when(level < layers - 1)
        def _():
            plane_copy(0, 1).wait_send()
            plane_copy(1, -1).wait_recv()

        @pl.when(level > 0)
        def _():
            plane_copy(1, -1).wait_send()
            plane_copy(0, 1).wait_recv()

        wide = 2 * REACH
        stacked = [halo[step, side, face] for face in range(4) for side in range(2)]
        parts = pool(jnp.concatenate(stacked, axis=0))
        spare = jnp.zeros((2 * wide, 128), BF16)
        sums = []
        gaps = []
        for face in range(4):
            rows = slice(opposite[face] * wide, (opposite[face] + 1) * wide)
            table = gather_table(*[part[rows] for part in parts]) + [spare]
            ghost = ghosts[face] + dot(halo_hot[face], jnp.concatenate(table, axis=0))
            sums.append(present[face] * (faces[face] + ghost))
            gaps.append(ghost - faces[face])
        for side, on, lift in ((0, low_on, -1.0), (1, high_on, 1.0)):
            ghost = ghost_planes[step, side]
            sums.append(on * (faces[4 + side] + ghost))
            gaps.append(ghost - faces[4 + side] + lift)
        push = []
        rim = []
        for first in range(0, 6, 2):
            here = pltpu.roll(sums[first], 64, 1)
            there = sums[first + 1]
            push.append(
                jnp.where(low, here * gaps[first], there * pltpu.roll(gaps[first + 1], 64, 1))
            )
            rim.append(jnp.where(low, here, there))
        push = jnp.concatenate(push, axis=1)
        rim = jnp.concatenate(rim, axis=1)
        if step == 0:
            spread = dot(jnp.concatenate([*split(push), *split(rim)], axis=0), t_put[...])
            diag = diag + spread[both : both + blocks] + spread[both + blocks :]
        else:
            spread = dot(jnp.concatenate(split(push), axis=0), t_put[...])
        return resid - (spread[:blocks] + spread[blocks:both]), diag

    start_head = settled_a[top_rows]

    def first_balance(flux, total):
        other_fields()
        alpha_here = settled_b[top_rows, seg[0]]
        n = settled_b[top_rows, seg[1]]
        root = closure(start_head, alpha_here, n, None)[0]
        resid = 4.0 * (water_of(root) - settled_b[end_rows, seg[2]]) - flux
        room = settled_b[end_rows, seg[1]] - settled_b[end_rows, seg[0]]
        return resid, 4.0 * room * alpha_here + total

    resid, diag = evaluate(0, start_head, settled_a[end_rows], first_balance)
    fresh = start_head - resid / diag
    new_head[0] = fresh
    root, conduct = closure(
        fresh, settled_b[top_rows, seg[0]], settled_b[top_rows, seg[1]], settled_b[top_rows, seg[2]]
    )

    def second_balance(flux, total):
        return 4.0 * (water_of(root) - settled_b[end_rows, seg[2]]) - flux, None

    residual[0] = evaluate(1, fresh, conduct, second_balance)[0]
    for copy in moves_a + moves_b:
        copy.wait_send()


def on_device(
    peers,
    layers,
    head,
    water_prev,
    alpha,
    shape_n,
    theta_r,
    theta_s,
    sat_cond,
    refine,
    destination,
    neighbours,
):
    blocks = head.shape[1]
    both = 2 * blocks
    slots = 8 * peers
    table = take_table()
    vmem = pl.BlockSpec(memory_space=pltpu.VMEM)
    hbm = pl.BlockSpec(memory_space=pltpu.HBM)
    dma = pltpu.SemaphoreType.DMA
    return pl.pallas_call(
        functools.partial(kernel, peers, layers),
        out_shape=(
            jax.ShapeDtypeStruct(head.shape, F32),
            jax.ShapeDtypeStruct(head.shape, F32),
        ),
        in_specs=[hbm] * 13,
        out_specs=(vmem, vmem),
        scratch_shapes=[pltpu.VMEM(head.shape, F32)] * 7
        + [
            pltpu.VMEM((1, blocks), jnp.int32),
            pltpu.VMEM((1, blocks), jnp.int32),
            pltpu.VMEM((4, 4, blocks), jnp.int32),
            pltpu.VMEM((CELLS, 384), BF16),
            pltpu.VMEM((384, CELLS), BF16),
            pltpu.VMEM((128, 128), BF16),
            dma((13,)),
            pltpu.VMEM((2 * both, 4 * CELLS), BF16),
            pltpu.VMEM((peers, 8, CELLS + 128), F32),
            pltpu.VMEM((peers, 8, 3 * CELLS), F32),
            pltpu.VMEM((peers, 8, CELLS + 128), F32),
            pltpu.VMEM((peers, 8, 3 * CELLS), F32),
            pltpu.VMEM((2 * both, CELLS), BF16),
            pltpu.VMEM((2 * both, 3 * CELLS), BF16),
            pltpu.VMEM((both, 2 * both), BF16),
            pltpu.VMEM((both, CELLS), F32),
            pltpu.VMEM((both, 3 * CELLS), F32),
            pltpu.VMEM((4, blocks, 640), BF16),
            pltpu.VMEM((4, blocks, 384), BF16),
            pltpu.VMEM((4, blocks, 128), F32),
            pltpu.VMEM((6, blocks, 128), F32),
            pltpu.VMEM((4, blocks, 128), F32),
            pltpu.VMEM((2, 2, 4, REACH, 128), F32),
            pltpu.VMEM((2, 2, blocks, 128), F32),
            dma((peers,)),
            dma((peers,)),
            dma((peers,)),
            dma((peers,)),
            dma((2, 2)),
            dma((2, 2)),
            dma((2, 2)),
            dma((2, 2)),
        ],
        compiler_params=pltpu.CompilerParams(
            collective_id=0, has_side_effects=True, vmem_limit_bytes=60 * 1024 * 1024
        ),
    )(
        head,
        water_prev,
        alpha,
        shape_n,
        theta_r,
        theta_s,
        sat_cond,
        refine.reshape(1, blocks),
        destination.reshape(1, blocks),
        neighbours.transpose(1, 2, 0),
        jnp.asarray(table, BF16),
        jnp.asarray(table.T, BF16),
        jnp.asarray(pool_table(), BF16),
    )


def solution(mesh):
    cells = P("depth", "dom", None)
    placed = (cells,) * 7 + (P("dom"), P("dom"), P("dom", None, None))
    return jax.shard_map(
        functools.partial(on_device, mesh.shape["dom"], mesh.shape["depth"]),
        mesh=mesh,
        in_specs=placed,
        out_specs=(cells, cells),
        check_vma=False,
    )
```

time: 23.4 us -> 21.5 us (0.919)
  Pallas kernels: 20.3 us -> 18.5 us
    pallas_call x1, Pallas kernels: 20.3 us -> 18.5 us  [on_device(): pl.pallas_call(functools.partial(kernel, peers, layers), out_shape=(jax.S...]
where the time goes in v4:
time: 21.5 us; the launch traced here: 21.4 us
  Pallas kernels  18.5 us (86%)
  local copies, waits for them, and re-layouts  2.26 us (11%)
  between operations  0.65 us (3%)
    pallas_call x1, Pallas kernels, on_device(): pl.pallas_call(functools.partial(kernel, peers, layers), out_shape=(jax.S...  18.5 us
    unnamed x4, local copies, waits for them, and re-layouts  2.26 us

profile of v4, /device:TPU:0, one launch (start us, length us, event | category | flops | bytes accessed | tf_op | source)
XLA Modules:
  0.0 21.4 jit_solution(7532579565186489034)
XLA Ops:
  0.6 18.5 %shard_map.140 = (f32[1,64,512]{2,1,0:T(8,128)}, f32[1,64,512]{2,1,0:T(8,128)}) custom-call(f32[1,64,512]{2,1,0:T(8,128)} %head_hbm.1, f32[1,64,512]{2,1,0:T(8,128)} %water_prev_hbm.1, f32[1,64,512]{2,1,0:T(8,128)} %alpha_hbm.1, f32[1,64,512]{2,1,0:T(8,128)} %shape_n_hbm.1, f32[1,64,512]{2,1,0:T(8,128)} %theta_r_hbm.1, f32[1,64,512]{2,1,0:T(8,128)} %theta_s_hbm.1, ...), custom_call_target="tpu_custom_call" | custom-call | tf_op jit(solution)/shard_map/pallas_call | solution.py:641
  19.1 0.0 copy-start
  19.1 1.6 %copy.17 = f32[1,64,512]{2,1,0:T(8,128)} copy(f32[1,64,512]{2,1,0:T(8,128)} %get-tuple-element.4) | data formatting | bytes 262144
  20.7 0.0 copy-done
  20.7 0.7 %copy.18 = f32[1,64,512]{2,1,0:T(8,128)} copy(f32[1,64,512]{2,1,0:T(8,128)S(1)} %copy-done) | data formatting | bytes 262144
Async XLA Ops:
  19.1 1.6 %copy-start = (f32[1,64,512]{2,1,0:T(8,128)S(1)}, f32[1,64,512]{2,1,0:T(8,128)}, u32[]{:S(2)}) copy-start(f32[1,64,512]{2,1,0:T(8,128)} %get-tuple-element.5) | copy-start | bytes 393220

commit v5 on v4

--- a/solution.py
+++ b/solution.py
@@ -342,7 +342,7 @@
                     device_id_type=MESH,
                 )
             )
-    for copy in moves_a + moves_b:
+    for copy in moves_a:
         copy.start()
 
     def put_rows(work, start, cols, value):
@@ -371,6 +371,8 @@
     hot = jnp.where(wanted, 1.0, 0.0).astype(BF16)
     place[...] = jnp.concatenate([hot, hot], axis=1)
     settled_a[...] = dot(place[...], work_a[...])
+    for copy in moves_b:
+        copy.start()
 
     for copy in loads[9:]:
         copy.wait()
@@ -617,6 +619,17 @@
         copy.wait_send()
 
 
+def hand_over(first, second, first_out, second_out, sem):
+    copies = [
+        pltpu.make_async_copy(first, first_out, sem.at[0]),
+        pltpu.make_async_copy(second, second_out, sem.at[1]),
+    ]
+    for copy in copies:
+        copy.start()
+    for copy in copies:
+        copy.wait()
+
+
 def on_device(
     peers,
     layers,
@@ -638,12 +651,13 @@
     vmem = pl.BlockSpec(memory_space=pltpu.VMEM)
     hbm = pl.BlockSpec(memory_space=pltpu.HBM)
     dma = pltpu.SemaphoreType.DMA
-    return pl.pallas_call(
+    out_shape = (
+        jax.ShapeDtypeStruct(head.shape, F32),
+        jax.ShapeDtypeStruct(head.shape, F32),
+    )
+    results = pl.pallas_call(
         functools.partial(kernel, peers, layers),
-        out_shape=(
-            jax.ShapeDtypeStruct(head.shape, F32),
-            jax.ShapeDtypeStruct(head.shape, F32),
-        ),
+        out_shape=out_shape,
         in_specs=[hbm] * 13,
         out_specs=(vmem, vmem),
         scratch_shapes=[pltpu.VMEM(head.shape, F32)] * 7
@@ -699,6 +713,14 @@
         jnp.asarray(table.T, BF16),
         jnp.asarray(pool_table(), BF16),
     )
+    return pl.pallas_call(
+        hand_over,
+        out_shape=out_shape,
+        in_specs=[hbm, hbm],
+        out_specs=(hbm, hbm),
+        scratch_shapes=[dma((2,))],
+        compiler_params=pltpu.CompilerParams(vmem_limit_bytes=60 * 1024 * 1024),
+    )(*results)
 
 
 def solution(mesh):

time: 21.5 us -> 28 us (1.30)
  Pallas kernels: 18.5 us -> 27.2 us
  local copies, waits for them, and re-layouts: 2.26 us -> 0 us
    pallas_call x1 -> x2, Pallas kernels: 18.5 us -> 27.2 us  [the longest x1 18.1 us: on_device(): pl.pallas_call(functools.partial(kernel, peers, layers), out_shape=out_sh...]
    unnamed x4 -> x0, local copies, waits for them, and re-layouts: 2.26 us -> none
where the time goes in v5:
time: 28 us; the launch traced here: 27.8 us
  Pallas kernels  27.2 us (97%)
  between operations  0.64 us (2%)
    pallas_call x1, Pallas kernels, on_device(): pl.pallas_call(functools.partial(kernel, peers, layers), out_shape=out_sh...  18.1 us
    pallas_call x1, Pallas kernels, on_device(): pl.pallas_call(hand_over, out_shape=out_shape, in_specs=[hbm, hbm], out_s...  9.06 us

profile of v5, /device:TPU:0, one launch (start us, length us, event | category | flops | bytes accessed | tf_op | source)
XLA Modules:
  0.0 27.8 jit_solution(5898502259465605220)
XLA Ops:
  0.6 18.1 %shard_map.140 = (f32[1,64,512]{2,1,0:T(8,128)}, f32[1,64,512]{2,1,0:T(8,128)}) custom-call(f32[1,64,512]{2,1,0:T(8,128)} %head_hbm.1, f32[1,64,512]{2,1,0:T(8,128)} %water_prev_hbm.1, f32[1,64,512]{2,1,0:T(8,128)} %alpha_hbm.1, f32[1,64,512]{2,1,0:T(8,128)} %shape_n_hbm.1, f32[1,64,512]{2,1,0:T(8,128)} %theta_r_hbm.1, f32[1,64,512]{2,1,0:T(8,128)} %theta_s_hbm.1, ...), custom_call_target="tpu_custom_call" | custom-call | tf_op jit(solution)/shard_map/pallas_call | solution.py:658
  18.8 9.1 %shard_map.141 = (f32[1,64,512]{2,1,0:T(8,128)}, f32[1,64,512]{2,1,0:T(8,128)}) custom-call(f32[1,64,512]{2,1,0:T(8,128)} %get-tuple-element.4.first, f32[1,64,512]{2,1,0:T(8,128)} %get-tuple-element.5.second), custom_call_target="tpu_custom_call" | custom-call | tf_op jit(solution)/shard_map/pallas_call | solution.py:716

commit v6 on v4

--- a/solution.py
+++ b/solution.py
@@ -159,8 +159,7 @@
     t_take_hbm,
     t_put_hbm,
     t_pool_hbm,
-    new_head,
-    residual,
+    results,
     head,
     water_prev,
     alpha,
@@ -342,7 +341,7 @@
                     device_id_type=MESH,
                 )
             )
-    for copy in moves_a + moves_b:
+    for copy in moves_a:
         copy.start()
 
     def put_rows(work, start, cols, value):
@@ -371,6 +370,8 @@
     hot = jnp.where(wanted, 1.0, 0.0).astype(BF16)
     place[...] = jnp.concatenate([hot, hot], axis=1)
     settled_a[...] = dot(place[...], work_a[...])
+    for copy in moves_b:
+        copy.start()
 
     for copy in loads[9:]:
         copy.wait()
@@ -604,7 +605,7 @@
 
     resid, diag = evaluate(0, start_head, settled_a[end_rows], first_balance)
     fresh = start_head - resid / diag
-    new_head[0] = fresh
+    results[top_rows] = fresh
     root, conduct = closure(
         fresh, settled_b[top_rows, seg[0]], settled_b[top_rows, seg[1]], settled_b[top_rows, seg[2]]
     )
@@ -612,7 +613,7 @@
     def second_balance(flux, total):
         return 4.0 * (water_of(root) - settled_b[end_rows, seg[2]]) - flux, None
 
-    residual[0] = evaluate(1, fresh, conduct, second_balance)[0]
+    results[end_rows] = evaluate(1, fresh, conduct, second_balance)[0]
     for copy in moves_a + moves_b:
         copy.wait_send()
 
@@ -638,14 +639,11 @@
     vmem = pl.BlockSpec(memory_space=pltpu.VMEM)
     hbm = pl.BlockSpec(memory_space=pltpu.HBM)
     dma = pltpu.SemaphoreType.DMA
-    return pl.pallas_call(
+    results = pl.pallas_call(
         functools.partial(kernel, peers, layers),
-        out_shape=(
-            jax.ShapeDtypeStruct(head.shape, F32),
-            jax.ShapeDtypeStruct(head.shape, F32),
-        ),
+        out_shape=jax.ShapeDtypeStruct((2 * blocks, CELLS), F32),
         in_specs=[hbm] * 13,
-        out_specs=(vmem, vmem),
+        out_specs=vmem,
         scratch_shapes=[pltpu.VMEM(head.shape, F32)] * 7
         + [
             pltpu.VMEM((1, blocks), jnp.int32),
@@ -699,6 +697,7 @@
         jnp.asarray(table.T, BF16),
         jnp.asarray(pool_table(), BF16),
     )
+    return results[:blocks][None], results[blocks:][None]
 
 
 def solution(mesh):

time: 21.5 us -> 20.6 us (0.958)
  local copies, waits for them, and re-layouts: 2.26 us -> 1.69 us
  Pallas kernels: 18.5 us -> 18.1 us
    unnamed x4 -> x0, local copies, waits for them, and re-layouts: 2.26 us -> none
    broadcast_in_dim x0 -> x1, local copies, waits for them, and re-layouts: none -> 1.69 us  [on_device(): return (results[:blocks][None], results[blocks:][None])]
    pallas_call x1, Pallas kernels: 18.5 us -> 18.1 us  [on_device(): pl.pallas_call(functools.partial(kernel, peers, layers), out_shape=jax.Sh...]
where the time goes in v6:
time: 20.6 us; the launch traced here: 20.5 us
  Pallas kernels  18.1 us (88%)
  local copies, waits for them, and re-layouts  1.69 us (8%)
  between operations  0.64 us (3%)
    pallas_call x1, Pallas kernels, on_device(): pl.pallas_call(functools.partial(kernel, peers, layers), out_shape=jax.Sh...  18.1 us
    broadcast_in_dim x1, local copies, waits for them, and re-layouts, on_device(): return (results[:blocks][None], results[blocks:][None])  1.69 us

profile of v6, /device:TPU:0, one launch (start us, length us, event | category | flops | bytes accessed | tf_op | source)
XLA Modules:
  0.0 20.5 jit_solution(15557824275736285979)
XLA Ops:
  0.6 18.1 %shard_map.140 = f32[128,512]{1,0:T(8,128)} custom-call(f32[1,64,512]{2,1,0:T(8,128)} %head_hbm.1, f32[1,64,512]{2,1,0:T(8,128)} %water_prev_hbm.1, f32[1,64,512]{2,1,0:T(8,128)} %alpha_hbm.1, f32[1,64,512]{2,1,0:T(8,128)} %shape_n_hbm.1, f32[1,64,512]{2,1,0:T(8,128)} %theta_r_hbm.1, f32[1,64,512]{2,1,0:T(8,128)} %theta_s_hbm.1, f32[1,64,512]{2,1,0:T(8,128)} %sat_cond_hbm.1, ...), custom_call_target="tpu_custom_call" | custom-call | tf_op jit(solution)/shard_map/pallas_call | solution.py:642
  18.8 1.7 %slice_bitcast_fusion = (f32[1,64,512]{2,1,0:T(8,128)}, f32[1,64,512]{2,1,0:T(8,128)}) fusion(f32[128,512]{1,0:T(8,128)} %shard_map.140), kind=kLoop, calls=%fused_computation | loop fusion | bytes 524288 | tf_op jit(solution)/shard_map/broadcast_in_dim | solution.py:700

commit v7 on v6

--- a/solution.py
+++ b/solution.py
@@ -246,23 +246,8 @@
     def _():
         pl.semaphore_signal(barrier, inc=1, device_id=(me, level + 1), device_id_type=MESH)
 
-    for copy in loads[:9]:
+    for copy in loads[:2]:
         copy.wait()
-    left = (head, alpha, shape_n, sat_cond)
-    right = (water_prev, theta_r, theta_s)
-    for s in range(4):
-        cols = pl.ds(s * CELLS, CELLS)
-        high, rest = split(left[s][0])
-        raw[pl.ds(0, blocks), cols] = high
-        raw[pl.ds(both, blocks), cols] = rest
-        if s < 3:
-            high, rest = split(right[s][0])
-            raw[pl.ds(blocks, blocks), cols] = high
-            raw[pl.ds(both + blocks, blocks), cols] = rest
-        else:
-            raw[pl.ds(blocks, blocks), cols] = jnp.zeros((blocks, CELLS), BF16)
-            raw[pl.ds(both + blocks, blocks), cols] = jnp.zeros((blocks, CELLS), BF16)
-
     dest = jnp.concatenate([destination[...], destination[...]], axis=1)
     flag_row = jnp.concatenate([refine[...], refine[...]], axis=1)
     owner = dest >> shift
@@ -290,6 +275,23 @@
     spot_sent = jnp.sum(hot * (spot + 1).astype(F32), axis=1, keepdims=True) - 1.0
     flag_sent = jnp.sum(hot * flag_row.astype(F32), axis=1, keepdims=True)
     hot = hot.astype(BF16)
+    for copy in loads[2:9]:
+        copy.wait()
+    left = (head, alpha, shape_n, sat_cond)
+    right = (water_prev, theta_r, theta_s)
+    for s in range(4):
+        cols = pl.ds(s * CELLS, CELLS)
+        high, rest = split(left[s][0])
+        raw[pl.ds(0, blocks), cols] = high
+        raw[pl.ds(both, blocks), cols] = rest
+        if s < 3:
+            high, rest = split(right[s][0])
+            raw[pl.ds(blocks, blocks), cols] = high
+            raw[pl.ds(both + blocks, blocks), cols] = rest
+        else:
+            raw[pl.ds(blocks, blocks), cols] = jnp.zeros((blocks, CELLS), BF16)
+            raw[pl.ds(both + blocks, blocks), cols] = jnp.zeros((blocks, CELLS), BF16)
+
     packed = dot(jnp.concatenate([hot, hot], axis=1), raw[...])
     filled = spot_sent >= 0.0
     for start in range(0, slots, 16):
@@ -540,23 +542,11 @@
 
         @pl.when(me < peers - 1)
         def _():
-            halo_copy(0, 1).wait_send()
             halo_copy(1, -1).wait_recv()
 
         @pl.when(me > 0)
         def _():
-            halo_copy(1, -1).wait_send()
             halo_copy(0, 1).wait_recv()
-
-        @pl.when(level < layers - 1)
-        def _():
-            plane_copy(0, 1).wait_send()
-            plane_copy(1, -1).wait_recv()
-
-        @pl.when(level > 0)
-        def _():
-            plane_copy(1, -1).wait_send()
-            plane_copy(0, 1).wait_recv()
 
         wide = 2 * REACH
         stacked = [halo[step, side, face] for face in range(4) for side in range(2)]
@@ -570,6 +560,15 @@
             ghost = ghosts[face] + dot(halo_hot[face], jnp.concatenate(table, axis=0))
             sums.append(present[face] * (faces[face] + ghost))
             gaps.append(ghost - faces[face])
+
+        @pl.when(level < layers - 1)
+        def _():
+            plane_copy(1, -1).wait_recv()
+
+        @pl.when(level > 0)
+        def _():
+            plane_copy(0, 1).wait_recv()
+
         for side, on, lift in ((0, low_on, -1.0), (1, high_on, 1.0)):
             ghost = ghost_planes[step, side]
             sums.append(on * (faces[4 + side] + ghost))
@@ -590,6 +589,23 @@
             diag = diag + spread[both : both + blocks] + spread[both + blocks :]
         else:
             spread = dot(jnp.concatenate(split(push), axis=0), t_put[...])
+
+        @pl.when(me < peers - 1)
+        def _():
+            halo_copy(0, 1).wait_send()
+
+        @pl.when(me > 0)
+        def _():
+            halo_copy(1, -1).wait_send()
+
+        @pl.when(level < layers - 1)
+        def _():
+            plane_copy(0, 1).wait_send()
+
+        @pl.when(level > 0)
+        def _():
+            plane_copy(1, -1).wait_send()
+
         return resid - (spread[:blocks] + spread[blocks:both]), diag
 
     start_head = settled_a[top_rows]

time: 20.6 us -> 20.4 us (level)
    pallas_call x1, Pallas kernels: 18.1 us -> 17.9 us  [on_device(): pl.pallas_call(functools.partial(kernel, peers, layers), out_shape=jax.Sh...]
where the time goes in v7:
time: 20.4 us; the launch traced here: 20.2 us
  Pallas kernels  17.9 us (88%)
  local copies, waits for them, and re-layouts  1.69 us (8%)
  between operations  0.64 us (3%)
    pallas_call x1, Pallas kernels, on_device(): pl.pallas_call(functools.partial(kernel, peers, layers), out_shape=jax.Sh...  17.9 us
    broadcast_in_dim x1, local copies, waits for them, and re-layouts, on_device(): return (results[:blocks][None], results[blocks:][None])  1.69 us

profile of v7, /device:TPU:0, one launch (start us, length us, event | category | flops | bytes accessed | tf_op | source)
XLA Modules:
  0.0 20.2 jit_solution(2669888412316793084)
XLA Ops:
  0.6 17.9 %shard_map.140 = f32[128,512]{1,0:T(8,128)} custom-call(f32[1,64,512]{2,1,0:T(8,128)} %head_hbm.1, f32[1,64,512]{2,1,0:T(8,128)} %water_prev_hbm.1, f32[1,64,512]{2,1,0:T(8,128)} %alpha_hbm.1, f32[1,64,512]{2,1,0:T(8,128)} %shape_n_hbm.1, f32[1,64,512]{2,1,0:T(8,128)} %theta_r_hbm.1, f32[1,64,512]{2,1,0:T(8,128)} %theta_s_hbm.1, f32[1,64,512]{2,1,0:T(8,128)} %sat_cond_hbm.1, ...), custom_call_target="tpu_custom_call" | custom-call | tf_op jit(solution)/shard_map/pallas_call | solution.py:658
  18.5 1.7 %slice_bitcast_fusion = (f32[1,64,512]{2,1,0:T(8,128)}, f32[1,64,512]{2,1,0:T(8,128)}) fusion(f32[128,512]{1,0:T(8,128)} %shard_map.140), kind=kLoop, calls=%fused_computation | loop fusion | bytes 524288 | tf_op jit(solution)/shard_map/broadcast_in_dim | solution.py:716
